TPU v7x, 128 devices: a whole 4x4x4 slice. The times are simulated.
128 devices in a mesh: kgrp: 4 (over z_hi, core), band: 32 (over x, z_lo, y).
Axes of the slice: x: 4, y: 4, z: 4 (z_hi: 2, z_lo: 2; z = z_hi * 2 + z_lo), core: 2. Of those that a mesh axis runs over, the one named last changes fastest.
Arguments:
- densities: bfloat16 [8, 128, 128, 4096], P('kgrp', 'band'), may hold values from -6 to 6
- amplitudes: bfloat16 [8, 8, 128, 128], P('kgrp'), may hold values from -0.046875 to 0.046875
- partner: int32 [8], replicated, may hold values from 0 to 7, as said below
- qtable: int32 [8], replicated, may hold values from 0 to 63
- grid_map: int32 [64, 4096], replicated, may hold values from 0 to 4095, each once within a row
- coulomb: float32 [64, 4096], replicated, may hold values from 0.5 to 2
Outputs:
- ladder: bfloat16 [128, 8, 8, 128], P('band', 'kgrp')
Inputs may be any that keep to these rules, and one draw needn't show every extreme that they name: partner is a permutation of the 8 k-pairs; k-pair r lies in group r // 2. The two pairs of a group have their partners in two different groups, neither of them the group itself, and the two pairs whose partners lie in one group belong to two different groups. `grid_map`: each row is a permutation of the 4096 grid positions.
All inputs are finite; a program needn't handle non-finite values.
Results may differ from a plain program's by a relative error of at most 0.0064.
Values may be sent and summed in bfloat16 or wider, within the bound.
No kernel may reach another device: no remote copies, remote signals or barrier semaphores. Data moves between devices by JAX's collectives and lax.ppermute only.
A program may use at most 192 MiB of HBM per device.

v0:
```python
import math

import jax
import jax.numpy as jnp
from jax import lax
from jax.sharding import PartitionSpec as P

G = 4096


def shards(densities, amplitudes, partner, qtable, grid_map, coulomb):
    my_group = lax.axis_index("kgrp")
    pair_count = densities.shape[0]
    own_ids = my_group * pair_count + jnp.arange(pair_count, dtype=jnp.int32)
    transfers = jnp.take(qtable, own_ids)
    positions = jnp.take(grid_map, transfers, axis=0)
    factors = jnp.take(coulomb, transfers, axis=0)
    picked = jax.vmap(lambda dens_block, grid_rows: jnp.take(dens_block, grid_rows, axis=2))(
        densities, positions
    )
    pre_vertex = (picked.astype(jnp.float32) * factors[:, None, None, :]).astype(jnp.bfloat16)
    vertex = lax.all_to_all(pre_vertex, "band", split_axis=3, concat_axis=1, tiled=True)
    partner_ids = jnp.take(partner, own_ids)
    everything = lax.all_gather(vertex, "kgrp", axis=0, tiled=True)
    right_blocks = jnp.take(everything, partner_ids, axis=0)
    pieces = []
    for pair_index in range(pair_count):
        left_pair = vertex[pair_index]
        right_pair = right_blocks[pair_index]

        def one_slab(amp_pair):
            mixed = jnp.einsum(
                "acg,cd->adg", left_pair, amp_pair, preferred_element_type=jnp.float32
            ).astype(jnp.bfloat16)
            return jnp.einsum("adg,bdg->ab", mixed, right_pair, preferred_element_type=jnp.float32)

        pieces.append(lax.map(one_slab, amplitudes[pair_index]))
    stacked = jnp.stack(pieces, axis=0)
    summed = lax.psum_scatter(
        jnp.transpose(stacked, (2, 0, 1, 3)), "band", scatter_dimension=0, tiled=True
    )
    return (summed * (1.0 / math.sqrt(G))).astype(jnp.bfloat16)


def solution(mesh):
    in_specs = (P("kgrp", "band", None, None), P("kgrp", None, None, None), P(), P(), P(), P())
    out_specs = P("band", "kgrp", None, None)
    return jax.shard_map(shards, mesh=mesh, in_specs=in_specs, out_specs=out_specs, check_vma=False)
```

profile of v0, /device:TPU:0, one launch (start us, length us, event | category | flops | bytes accessed | tf_op | source)
XLA Modules:
  0.0 800.8 jit_solution(11672637812101279798)
XLA Ops:
  8.8 13.7 %copy.34 = bf16[2,4,128,4096]{2,1,3,0:T(4,128)(2,1)} copy(bf16[2,4,128,4096]{3,2,1,0:T(8,128)(2,1)} %param.12) | data formatting | bytes 16777216 | tf_op args[0]
  25.9 71.6 %gather_fusion.2 = bf16[8192,4,128]{2,1,0:T(4,128)(2,1)} fusion(bf16[2,4,128,4096]{2,1,3,0:T(4,128)(2,1)} %copy.34, s32[8192]{0:T(1024)S(1)} %bitcast.77), kind=kCustom, calls=%fused_computation.4 | custom fusion | bytes 16842752 | tf_op jit(solution)/shard_map/vmap(jit(_take))/gather | solution.py:18
  97.6 21.0 %fusion.10 = bf16[2,4,128,4096]{2,1,0,3:T(4,128)(2,1)S(1)} fusion(bf16[2,4096,4,128]{3,2,1,0:T(4,128)(2,1)} %bitcast.82, f32[2,4096]{0,1:T(8,128)S(1)} %copy.36, pred[2,4096]{0,1:T(8,128)(4,1)S(1)} %copy.33), kind=kLoop, calls=%fused_computation.20 | loop fusion | flops 16777216 | bytes 16818176 | tf_op jit(solution)/shard_map/convert_element_type | solution.py:21
  118.6 103.8 %all_to_all.18 = bf16[2,4,128,4096]{2,1,0,3:T(4,128)(2,1)} all-to-all(bf16[2,4,128,4096]{2,1,0,3:T(4,128)(2,1)S(1)} %fusion.10), channel_id=1, replica_groups=mesh['kgrp'=4,'band'=32] {'band'}, dimensions={3} | all-to-all | bytes 16777216 | tf_op jit(solution)/shard_map/all_to_all | solution.py:22
  222.4 7.7 copy.37
  230.1 12.0 %copy.39 = bf16[2,32,4,128,128]{4,3,2,1,0:T(8,128)(2,1)} copy(bf16[2,32,4,128,128]{3,4,1,2,0:T(8,128)(2,1)} %bitcast.80) | data formatting | bytes 16777216 | tf_op jit(solution)/shard_map/all_to_all | solution.py:22
  243.8 6.1 fusion.15
  250.0 7.1 copy.38
  257.1 6.9 copy.43
  264.0 183.1 %all-gather.2.cloned.1.call-done = bf16[8,128,128,128]{3,2,1,0:T(8,128)(2,1)} async-done(((bf16[2,128,128,128]{3,2,1,0:T(8,128)(2,1)}), bf16[8,128,128,128]{3,2,1,0:T(8,128)(2,1)}) %all-gather.2.cloned.1.call-update) | async-done | bytes 33554448 | tf_op jit(solution)/shard_map/all_gather | solution.py:24
  447.1 12.2 %while.23 = (s32[]{:T(128)}, bf16[8,128,128,128]{3,2,1,0:T(8,128)(2,1)}, s32[2,1]{0,1:T(1,128)S(1)}, bf16[2,128,128,128]{3,2,1,0:T(8,128)(2,1)}, s32[]{:T(128)}) while((s32[]{:T(128)}, bf16[8,128,128,128]{3,2,1,0:T(8,128)(2,1)}, s32[2,1]{0,1:T(1,128)S(1)}, bf16[2,128,128,128]{3,2,1,0:T(8,128)(2,1)}, s32[]{:T(128)}) %tuple.73), condition=%wide.while_cond, body=%wide.while_body.sunk | while | flops 2 | bytes 8389705 | solution.py:25
  447.8 5.5 dynamic-slice_dynamic-update-slice_fusion.2
  453.9 5.4 dynamic-slice_dynamic-update-slice_fusion.2
  459.3 7.5 broadcast_select_fusion
  466.8 5.2 slice_bitcast_fusion.1
  472.1 4.7 copy.40
  476.8 73.8 %while.21 = (s32[]{:T(128)}, f32[8,128,128]{2,0,1:T(8,128)S(1)}, bf16[8,128,128]{1,2,0:T(8,128)(2,1)S(1)}, bf16[128,128,128]{2,1,0:T(8,128)(2,1)}, bf16[128,128,128]{2,0,1:T(8,128)(2,1)}, /*index=5*/s32[]{:T(128)}, s32[]{:T(128)}) while((s32[]{:T(128)}, f32[8,128,128]{2,0,1:T(8,128)S(1)}, bf16[8,128,128]{1,2,0:T(8,128)(2,1)S(1)}, ...), condition=%wide.region_1.3_spmd, body=%wide.region_0.0_spmd.sunk | while | flops 1075838976 | bytes 33783920 | solution.py:37
  480.4 4.1 fusion.35
  489.6 4.1 fusion.35
  498.8 4.1 fusion.35
  508.0 4.1 fusion.35
  517.2 4.1 fusion.35
  526.4 4.1 fusion.35
  535.6 4.1 fusion.35
  544.8 4.1 fusion.35
  550.6 6.9 copy.44
  557.5 73.6 %while.22 = (s32[]{:T(128)}, f32[8,128,128]{2,0,1:T(8,128)S(1)}, bf16[8,128,128]{1,2,0:T(8,128)(2,1)S(1)}, bf16[128,128,128]{2,1,0:T(8,128)(2,1)}, bf16[128,128,128]{2,0,1:T(8,128)(2,1)}, /*index=5*/s32[]{:T(128)}, s32[]{:T(128)}) while((s32[]{:T(128)}, f32[8,128,128]{2,0,1:T(8,128)S(1)}, bf16[8,128,128]{1,2,0:T(8,128)(2,1)S(1)}, ...), condition=%wide.region_3.5_spmd, body=%wide.region_2.4_spmd.sunk | while | flops 1075838976 | bytes 33783920 | solution.py:37
  597.9 4.1 fusion.40
  607.1 4.1 fusion.40
  616.3 4.1 fusion.40
  625.4 4.1 fusion.40
  632.1 160.4 %reduce-scatter.2.cloned.1.call-done = f32[4,2,8,128]{3,2,1,0:T(8,128)} async-done(((f32[128,2,8,128]{3,2,1,0:T(8,128)}), f32[4,2,8,128]{3,2,1,0:T(8,128)}) %reduce-scatter.2.cloned.1.call-update) | async-done | bytes 32784 | tf_op jit(solution)/shard_map/reduce_scatter | solution.py:39
  (105 shorter events, 107.9 us)
Async XLA Ops:
  6.5 1.4 copy-start
  6.5 440.6 %all-gather.2.cloned.1.call-start = ((), (), s32[]{:S(2)}) async-start(), calls=%async_computation.2 | async-start | bytes 41943040 | tf_op jit(solution)/shard_map/all_gather | solution.py:24
  242.1 0.7 copy-start.2
  242.1 1.3 copy-start.5
  242.1 550.4 %reduce-scatter.2.cloned.1.call-start = ((), (), s32[]{:S(2)}) async-start(), calls=%async_computation.3 | async-start | bytes 1081344 | tf_op jit(solution)/shard_map/reduce_scatter | solution.py:39
  476.8 3.6 copy-start.4
  486.0 3.6 copy-start.4
  495.2 3.6 copy-start.4
  504.4 3.6 copy-start.4
  513.6 3.6 copy-start.4
  522.8 3.6 copy-start.4
  532.0 3.6 copy-start.4
  541.2 3.6 copy-start.4
  557.5 3.6 copy-start.3
  566.7 3.6 copy-start.3
  575.9 3.6 copy-start.3
  585.1 3.6 copy-start.3
  594.3 3.6 copy-start.3
  603.4 3.6 copy-start.3
  612.6 3.6 copy-start.3
  621.8 3.6 copy-start.3
  631.0 162.9 %copy-start.1 = (s32[64,4096]{1,0:T(8,128)S(1)}, s32[64,4096]{1,0:T(8,128)}, u32[]{:S(2)}) copy-start(s32[64,4096]{1,0:T(8,128)} %param.16) | copy-start | bytes 3145732
Sparse Core Ops, SparseCore 0:
  242.2 204.8 all-gather.1
  632.2 160.2 reduce-scatter.1
where the time goes:
time: 802 us; the launch traced here: 801 us
  waiting for transfers between devices  344 us (43%)
  local copies, waits for them, and re-layouts  184 us (23%)
  matrix products  123 us (15%)
  blocking collectives  104 us (13%)
  other arithmetic  31.3 us (4%)
  between operations  13.5 us (2%)
    all_gather x1, waiting for transfers between devices, shards(): everything = lax.all_gather(vertex, 'kgrp', axis=0, tiled=True)  183 us
    reduce_scatter x1, waiting for transfers between devices, shards(): lax.psum_scatter(jnp.transpose(stacked, (2, 0, 1, 3)), 'band', scatter_di...  160 us
    all_to_all x1, blocking collectives, shards(): lax.all_to_all(pre_vertex, 'band', split_axis=3, concat_axis=1, tiled=True)  104 us
    gather x1, local copies, waits for them, and re-layouts, shards(): jnp.take(dens_block, grid_rows, axis=2)  71.6 us
    dot_general x16, matrix products, one_slab(): jnp.einsum('adg,bdg->ab', mixed, right_pair, preferred_element_type=jnp.f...  65.9 us
    dot_general x16, matrix products, one_slab(): jnp.einsum('acg,cd->adg', left_pair, amp_pair, preferred_element_type=jnp...  57.3 us
    dynamic_update_slice x16, local copies, waits for them, and re-layouts, shards(): pieces.append(lax.map(one_slab, amplitudes[pair_index]))  23 us
    convert_element_type x1, other arithmetic, shards(): (picked.astype(jnp.float32) * factors[:, None, None, :]).astype(jnp.bfloa...  21 us
  transfers between devices with their start and end apart: 2, of which 2 were waited for; matrix products, arithmetic and copies ran while one was open for 3% of the time, Pallas kernels for 0%

commit v1 on v0

v1 whole, which is shorter than its diff:
```python
import functools
import math

import jax
import jax.numpy as jnp
from jax import lax
from jax.experimental import pallas as pl
from jax.experimental.pallas import tpu as pltpu
from jax.sharding import PartitionSpec as P

G = 4096
AXES = ("kgrp", "band")
CHUNKS = 4
GC = 32 // CHUNKS
BLOCK = 512
BF, F32 = jnp.bfloat16, jnp.float32


def column(row):
    return jnp.transpose(jnp.broadcast_to(row, (128, 128)), (1, 0))


def gather_kernel(map_ref, coul_ref, dens_ref, out_ref, onehot):
    lane = lax.broadcasted_iota(jnp.int32, (128, 128), 1)
    for b in range(BLOCK // 128):
        col = column(map_ref[0, 0, b : b + 1, :])
        high = (col >> 7).astype(F32).astype(BF)
        low = jnp.where((col & 127) == lane, 1.0, 0.0).astype(BF)
        zero = jnp.zeros_like(low)
        for kb in range(G // 128):
            onehot[b * 128 : (b + 1) * 128, kb * 128 : (kb + 1) * 128] = jnp.where(
                high == jnp.asarray(kb, BF), low, zero
            )
    picked = lax.dot_general(
        onehot[...], dens_ref[0], (((1,), (1,)), ((), ())), preferred_element_type=F32
    )
    n = 128 // GC
    for b in range(BLOCK // 128):
        factor = column(coul_ref[0, 0, b : b + 1, :])
        for l in range(4):
            scaled = picked[b * 128 : (b + 1) * 128, l * 128 : (l + 1) * 128] * factor
            out_ref[b * n : (b + 1) * n, 0, :, l * 128 : (l + 1) * 128] = scaled.reshape(n, GC, 128).astype(BF)


def gather(dens, maps, couls):
    steps = 128 * GC // BLOCK
    small = pl.BlockSpec((1, 1, BLOCK // 128, 128), lambda r, i: (r, i, 0, 0))
    return pl.pallas_call(
        gather_kernel,
        grid=(2, steps),
        in_specs=[small, small, pl.BlockSpec((1, 512, G), lambda r, i: (r, 0, 0))],
        out_specs=pl.BlockSpec((BLOCK // GC, 1, GC, 512), lambda r, i: (i, r, 0, 0)),
        out_shape=jax.ShapeDtypeStruct((128, 2, GC, 512), BF),
        scratch_shapes=[pltpu.VMEM((BLOCK, G), BF)],
        compiler_params=pltpu.CompilerParams(vmem_limit_bytes=60 * 2**20),
        cost_estimate=pl.CostEstimate(flops=4 * 128 * GC * G * 512, bytes_accessed=10**7, transcendentals=0),
        name="vertex_rows",
    )(maps.reshape(2, steps, BLOCK // 128, 128), couls.reshape(2, steps, BLOCK // 128, 128), dens)


def ladder_kernel(first, last, partner_ref, recv_ref, amp_ref, *refs):
    refs = list(refs)
    acc_in = None if first else refs.pop(0)
    out_ref, vert, mixed, wide = refs[:4]
    r = pl.program_id(0)

    @pl.when(r == 0)
    def _():
        for k in range(4):
            for r2 in range(2):
                for h in range(GC // 8):
                    for a4 in range(4):
                        wide[a4] = (
                            recv_ref[k, :, r2, h * 8 : (h + 1) * 8, a4 * 128 : (a4 + 1) * 128]
                            .astype(F32)
                            .reshape(256, 128)
                        )
                    for g in range(8):
                        for a4 in range(4):
                            vert[2 * k + r2, h * 8 + g, a4 * 32 : (a4 + 1) * 32, :] = wide[
                                a4, pl.ds(g, 32, stride=8), :
                            ].astype(BF)

    left = vert[r].reshape(GC * 128, 128)
    for p in range(4):
        amp = jnp.concatenate([amp_ref[0, 2 * p], amp_ref[0, 2 * p + 1]], axis=1)
        m = jnp.dot(left, amp, preferred_element_type=F32).astype(BF)
        for i in range(2):
            for g in range(GC):
                mixed[(2 * p + i) * 128 : (2 * p + i + 1) * 128, g * 128 : (g + 1) * 128] = m[
                    g * 128 : (g + 1) * 128, i * 128 : (i + 1) * 128
                ]
    w = vert[partner_ref[r]]
    right = jnp.concatenate([w[g] for g in range(GC)], axis=1)
    res = lax.dot_general(mixed[...], right, (((1,), (1,)), ((), ())), preferred_element_type=F32)
    if not first:
        res = res + acc_in[0]
    if last:
        total = refs[4]
        total[...] = res
        for s in range(32):
            out_ref[0, s, 0, :, :] = total[pl.ds(s, 32, stride=32), :].astype(BF)
    else:
        out_ref[0] = res


def ladder(partner, recv, amp, acc, last):
    ins = [
        pl.BlockSpec((4, 32, 2, GC, 512), lambda r, p: (0, 0, 0, 0, 0)),
        pl.BlockSpec((1, 8, 128, 128), lambda r, p: (r, 0, 0, 0)),
    ]
    args = [partner, recv.reshape(4, 32, 2, GC, 512), amp]
    if acc is not None:
        ins.append(pl.BlockSpec((1, 1024, 128), lambda r, p: (r, 0, 0)))
        args.append(acc)
    scratch = [
        pltpu.VMEM((8, GC, 128, 128), BF),
        pltpu.VMEM((1024, GC * 128), BF),
        pltpu.VMEM((4, 256, 128), F32),
    ]
    if last:
        out_spec = pl.BlockSpec((1, 32, 1, 32, 128), lambda r, p: (r // 2, 0, r % 2, 0, 0))
        out_shape = jax.ShapeDtypeStruct((4, 32, 2, 32, 128), BF)
        scratch.append(pltpu.VMEM((1024, 128), F32))
    else:
        out_spec = pl.BlockSpec((1, 1024, 128), lambda r, p: (r, 0, 0))
        out_shape = jax.ShapeDtypeStruct((8, 1024, 128), F32)
    return pl.pallas_call(
        functools.partial(ladder_kernel, acc is None, last),
        grid_spec=pltpu.PrefetchScalarGridSpec(
            num_scalar_prefetch=1, grid=(8,), in_specs=ins, out_specs=out_spec, scratch_shapes=scratch
        ),
        out_shape=out_shape,
        compiler_params=pltpu.CompilerParams(vmem_limit_bytes=60 * 2**20),
        cost_estimate=pl.CostEstimate(flops=32 * 8 * 128**3 * GC // 8 * 8, bytes_accessed=12 * 10**6, transcendentals=0),
        name="ladder_sum",
    )(*args)


def shards(densities, amplitudes, partner, qtable, grid_map, coulomb):
    own = lax.axis_index("kgrp") * 2
    amp = lax.all_gather(amplitudes, "kgrp", axis=0, tiled=True)
    rows = [qtable[own + i] for i in range(2)]
    maps = jnp.concatenate([lax.dynamic_slice_in_dim(grid_map, q, 1, 0) for q in rows], axis=0)
    couls = jnp.concatenate([lax.dynamic_slice_in_dim(coulomb, q, 1, 0) for q in rows], axis=0)
    dens = densities.reshape(2, 512, G)
    width = 128 * GC
    received = []
    for q in range(CHUNKS):
        part = slice(q * width, (q + 1) * width)
        sent = gather(dens, maps[:, part], couls[:, part])
        received.append(lax.all_to_all(sent, AXES, 0, 0, tiled=True))
    acc = None
    for q in range(CHUNKS):
        acc = ladder(partner, received[q], amp, acc, q == CHUNKS - 1)
    parts = lax.all_to_all(acc.reshape(128, 64, 128), AXES, 0, 0, tiled=True)
    total = jnp.sum(parts.astype(F32), axis=0) * (1.0 / math.sqrt(G))
    total = total.astype(BF).reshape(2, 8, 4, 4, 32)
    return jnp.transpose(total, (2, 0, 1, 4, 3)).reshape(4, 2, 8, 128)


def solution(mesh):
    in_specs = (P("kgrp", "band", None, None), P("kgrp", None, None, None), P(), P(), P(), P())
    out_specs = P("band", "kgrp", None, None)
    return jax.shard_map(shards, mesh=mesh, in_specs=in_specs, out_specs=out_specs, check_vma=False)
```

time: 802 us -> 268 us (0.33)
  waiting for transfers between devices: 344 us -> 49 us
  local copies, waits for them, and re-layouts: 184 us -> 12 us
  matrix products: 123 us -> 0 us
  Pallas kernels: 0 us -> 121 us
  blocking collectives: 104 us -> 40 us
  other arithmetic: 31.3 us -> 0.44 us
  starting transfers between devices: 0.22 us -> 27.5 us
    all_gather x1, waiting for transfers between devices: 183 us -> 0.02 us  [shards(): amp = lax.all_gather(amplitudes, 'kgrp', axis=0, tiled=True)]
    reduce_scatter x1 -> x0, waiting for transfers between devices: 160 us -> none  [shards(): lax.psum_scatter(jnp.transpose(stacked, (2, 0, 1, 3)), 'band', scatter_di...]
    dot_general x32 -> x0, matrix products: 123 us -> none  [the longest x16 65.9 us: one_slab(): jnp.einsum('adg,bdg->ab', mixed, right_pair, preferred_element_type=jnp.f...]
    pallas_call x0 -> x8, Pallas kernels: none -> 121 us  [the longest x4 69.2 us: ladder(): pl.pallas_call(functools.partial(ladder_kernel, acc is None, last), grid_...]
    gather x9 -> x0, local copies, waits for them, and re-layouts: 88.3 us -> none  [the longest x1 71.6 us: shards(): jnp.take(dens_block, grid_rows, axis=2)]
    all_to_all x1, blocking collectives: 104 us -> 40 us  [shards(): parts = lax.all_to_all(acc.reshape(128, 64, 128), AXES, 0, 0, tiled=True)]
    all_to_all x0 -> x4, waiting for transfers between devices: none -> 48.3 us  [shards(): received.append(lax.all_to_all(sent, AXES, 0, 0, tiled=True))]
    all_to_all x0 -> x4, starting transfers between devices: none -> 27.5 us  [shards(): received.append(lax.all_to_all(sent, AXES, 0, 0, tiled=True))]
  transfers between devices with their start and end apart: 2 -> 5, of which waited for: 2 -> 3; matrix products, arithmetic and copies ran while one was open for 3% -> 1% of each run, Pallas kernels for 0% -> 33%
where the time goes in v1:
time: 268 us; the launch traced here: 267 us
  Pallas kernels  121 us (45%)
  waiting for transfers between devices  49 us (18%)
  blocking collectives  40 us (15%)
  starting transfers between devices  27.5 us (10%)
  between operations  17.3 us (6%)
  local copies, waits for them, and re-layouts  12 us (4%)
    pallas_call x4, Pallas kernels, ladder(): pl.pallas_call(functools.partial(ladder_kernel, acc is None, last), grid_...  69.2 us
    pallas_call x4, Pallas kernels, gather(): pl.pallas_call(gather_kernel, grid=(2, steps), in_specs=[small, small, pl...  51.4 us
    all_to_all x4, waiting for transfers between devices, shards(): received.append(lax.all_to_all(sent, AXES, 0, 0, tiled=True))  48.3 us
    all_to_all x1, blocking collectives, shards(): parts = lax.all_to_all(acc.reshape(128, 64, 128), AXES, 0, 0, tiled=True)  40 us
    all_to_all x4, starting transfers between devices, shards(): received.append(lax.all_to_all(sent, AXES, 0, 0, tiled=True))  27.5 us
  transfers between devices with their start and end apart: 5, of which 3 were waited for; matrix products, arithmetic and copies ran while one was open for 1% of the time, Pallas kernels for 33%

profile of v1, /device:TPU:0, one launch (start us, length us, event | category | flops | bytes accessed | tf_op | source)
XLA Modules:
  0.0 266.8 jit_solution(3799795049891524400)
XLA Ops:
  6.5 1.4 fusion.6
  11.7 1.0 constant_dynamic-slice_fusion
  12.8 0.6 reshape.61.coul_ref
  13.4 1.0 constant_dynamic-slice_fusion.2
  14.4 0.6 reshape.60.map_ref
  15.0 12.8 %vertex_rows.7 = bf16[128,2,8,512]{3,2,1,0:T(8,128)(2,1)} custom-call(s32[2,2,4,128]{3,2,1,0:T(4,128)} %reshape.60.map_ref, f32[2,2,4,128]{3,2,1,0:T(4,128)} %reshape.61.coul_ref, bf16[2,512,4096]{2,1,0:T(8,128)(2,1)} %bitcast.15), custom_call_target="tpu_custom_call" | custom-call | flops 8589934592 | bytes 10000000 | tf_op jit(solution)/shard_map/vertex_rows/pallas_call | solution.py:48
  27.9 11.1 %all-to-all-start.3 = ((bf16[128,2,8,512]{3,2,1,0:T(8,128)(2,1)}), bf16[128,2,8,512]{3,2,1,0:T(8,128)(2,1)S(1)}, u32[]{:S(2)}, u32[]{:S(2)}) async-start(bf16[128,2,8,512]{3,2,1,0:T(8,128)(2,1)} %vertex_rows.7), calls=%async_computation.3 | async-start | bytes 4194304 | tf_op jit(solution)/shard_map/all_to_all | solution.py:152
  39.0 0.6 reshape.58.coul_ref
  39.6 0.6 reshape.57.map_ref
  40.2 12.9 %vertex_rows.6 = bf16[128,2,8,512]{3,2,1,0:T(8,128)(2,1)} custom-call(s32[2,2,4,128]{3,2,1,0:T(4,128)} %reshape.57.map_ref, f32[2,2,4,128]{3,2,1,0:T(4,128)} %reshape.58.coul_ref, bf16[2,512,4096]{2,1,0:T(8,128)(2,1)} %bitcast.16), custom_call_target="tpu_custom_call" | custom-call | flops 8589934592 | bytes 10000000 | tf_op jit(solution)/shard_map/vertex_rows/pallas_call | solution.py:48
  53.1 16.3 %all-to-all-done.3 = bf16[128,2,8,512]{3,2,1,0:T(8,128)(2,1)S(1)} async-done(((bf16[128,2,8,512]{3,2,1,0:T(8,128)(2,1)}), bf16[128,2,8,512]{3,2,1,0:T(8,128)(2,1)S(1)}, u32[]{:S(2)}, u32[]{:S(2)}) %all-to-all-start.3) | async-done | bytes 2097184 | tf_op jit(solution)/shard_map/all_to_all | solution.py:152
  69.4 1.3 copy-done
  70.8 5.8 %all-to-all-start.2 = ((bf16[128,2,8,512]{3,2,1,0:T(8,128)(2,1)}), bf16[128,2,8,512]{3,2,1,0:T(8,128)(2,1)}, u32[]{:S(2)}, u32[]{:S(2)}) async-start(bf16[128,2,8,512]{3,2,1,0:T(8,128)(2,1)} %vertex_rows.6), calls=%async_computation.2 | async-start | bytes 4194304 | tf_op jit(solution)/shard_map/all_to_all | solution.py:152
  76.6 0.7 all-gather.2.cloned.1.call-update
  77.3 0.6 reshape.55.coul_ref
  77.9 0.6 reshape.54.map_ref
  78.5 12.8 %vertex_rows.5 = bf16[128,2,8,512]{3,2,1,0:T(8,128)(2,1)} custom-call(s32[2,2,4,128]{3,2,1,0:T(4,128)} %reshape.54.map_ref, f32[2,2,4,128]{3,2,1,0:T(4,128)} %reshape.55.coul_ref, bf16[2,512,4096]{2,1,0:T(8,128)(2,1)} %bitcast.17), custom_call_target="tpu_custom_call" | custom-call | flops 8589934592 | bytes 10000000 | tf_op jit(solution)/shard_map/vertex_rows/pallas_call | solution.py:48
  91.4 15.6 %all-to-all-done.2 = bf16[128,2,8,512]{3,2,1,0:T(8,128)(2,1)} async-done(((bf16[128,2,8,512]{3,2,1,0:T(8,128)(2,1)}), bf16[128,2,8,512]{3,2,1,0:T(8,128)(2,1)}, u32[]{:S(2)}, u32[]{:S(2)}) %all-to-all-start.2) | async-done | bytes 2097184 | tf_op jit(solution)/shard_map/all_to_all | solution.py:152
  107.0 4.6 %all-to-all-start.1 = ((bf16[128,2,8,512]{3,2,1,0:T(8,128)(2,1)}), bf16[128,2,8,512]{3,2,1,0:T(8,128)(2,1)S(1)}, u32[]{:S(2)}, u32[]{:S(2)}) async-start(bf16[128,2,8,512]{3,2,1,0:T(8,128)(2,1)} %vertex_rows.5), calls=%async_computation.1 | async-start | bytes 4194304 | tf_op jit(solution)/shard_map/all_to_all | solution.py:152
  111.6 0.6 reshape.51.coul_ref
  112.3 0.6 reshape.50.map_ref
  112.9 12.8 %vertex_rows.4 = bf16[128,2,8,512]{3,2,1,0:T(8,128)(2,1)} custom-call(s32[2,2,4,128]{3,2,1,0:T(4,128)} %reshape.50.map_ref, f32[2,2,4,128]{3,2,1,0:T(4,128)} %reshape.51.coul_ref, bf16[2,512,4096]{2,1,0:T(8,128)(2,1)} %bitcast.18), custom_call_target="tpu_custom_call" | custom-call | flops 8589934592 | bytes 10000000 | tf_op jit(solution)/shard_map/vertex_rows/pallas_call | solution.py:48
  125.7 16.4 %all-to-all-done.1 = bf16[128,2,8,512]{3,2,1,0:T(8,128)(2,1)S(1)} async-done(((bf16[128,2,8,512]{3,2,1,0:T(8,128)(2,1)}), bf16[128,2,8,512]{3,2,1,0:T(8,128)(2,1)S(1)}, u32[]{:S(2)}, u32[]{:S(2)}) %all-to-all-start.1) | async-done | bytes 2097184 | tf_op jit(solution)/shard_map/all_to_all | solution.py:152
  142.1 1.3 copy-done.1
  143.4 6.0 %all-to-all-start = ((bf16[128,2,8,512]{3,2,1,0:T(8,128)(2,1)}), bf16[128,2,8,512]{3,2,1,0:T(8,128)(2,1)}, u32[]{:S(2)}, u32[]{:S(2)}) async-start(bf16[128,2,8,512]{3,2,1,0:T(8,128)(2,1)} %vertex_rows.4), calls=%async_computation | async-start | bytes 4194304 | tf_op jit(solution)/shard_map/all_to_all | solution.py:152
  149.4 16.6 %ladder_sum.4.refs_0_ = f32[8,1024,128]{2,1,0:T(8,128)} custom-call(s32[8]{0:T(128)} %partner_ref.7, bf16[4,32,2,8,512]{4,3,2,1,0:T(8,128)(2,1)} %bitcast.10, bf16[8,8,128,128]{3,2,1,0:T(8,128)(2,1)} %all-gather.2.cloned.1.call-done.amp_ref), custom_call_target="tpu_custom_call" | custom-call | flops 4294967296 | bytes 12000000 | tf_op jit(solution)/shard_map/ladder_sum/pallas_call | solution.py:128
  166.0 16.8 %ladder_sum.5.refs_0_ = f32[8,1024,128]{2,1,0:T(8,128)} custom-call(s32[8]{0:T(128)} %partner_ref.7, bf16[4,32,2,8,512]{4,3,2,1,0:T(8,128)(2,1)} %bitcast.5.recv_ref, bf16[8,8,128,128]{3,2,1,0:T(8,128)(2,1)} %all-gather.2.cloned.1.call-done.amp_ref, f32[8,1024,128]{2,1,0:T(8,128)} %ladder_sum.4.refs_0_), custom_call_target="tpu_custom_call" | custom-call | flops 4294967296 | bytes 12000000 | tf_op jit(solution)/shard_map/ladder_sum/pallas_call | solution.py:128
  182.8 16.8 %ladder_sum.6.refs_0_ = f32[8,1024,128]{2,1,0:T(8,128)} custom-call(s32[8]{0:T(128)} %partner_ref.7, bf16[4,32,2,8,512]{4,3,2,1,0:T(8,128)(2,1)} %bitcast.11, bf16[8,8,128,128]{3,2,1,0:T(8,128)(2,1)} %all-gather.2.cloned.1.call-done.amp_ref, f32[8,1024,128]{2,1,0:T(8,128)} %ladder_sum.5.refs_0_), custom_call_target="tpu_custom_call" | custom-call | flops 4294967296 | bytes 12000000 | tf_op jit(solution)/shard_map/ladder_sum/pallas_call | solution.py:128
  199.6 19.0 %ladder_sum.7 = bf16[4,32,2,32,128]{4,3,2,1,0:T(8,128)(2,1)} custom-call(s32[8]{0:T(128)} %partner_ref.7, bf16[4,32,2,8,512]{4,3,2,1,0:T(8,128)(2,1)} %bitcast.3.recv_ref, bf16[8,8,128,128]{3,2,1,0:T(8,128)(2,1)} %all-gather.2.cloned.1.call-done.amp_ref, f32[8,1024,128]{2,1,0:T(8,128)} %ladder_sum.6.refs_0_), custom_call_target="tpu_custom_call" | custom-call | flops 4294967296 | bytes 12000000 | tf_op jit(solution)/shard_map/ladder_sum/pallas_call | solution.py:128
  218.6 40.0 %all_to_all.25 = bf16[128,64,128]{2,1,0:T(8,128)(2,1)S(1)} all-to-all(bf16[128,64,128]{2,1,0:T(8,128)(2,1)} %bitcast.12), channel_id=1, replica_groups=mesh['kgrp'=4,'band'=32] {'kgrp','band'}, dimensions={0} | all-to-all | bytes 4194304 | tf_op jit(solution)/shard_map/all_to_all | solution.py:156
  258.6 0.4 convert_reduce_fusion
  259.3 0.7 copy.10
  (10 shorter events, 0.4 us)
Async XLA Ops:
  27.9 41.6 %all-to-all-start.3 = ((bf16[128,2,8,512]{3,2,1,0:T(8,128)(2,1)}), bf16[128,2,8,512]{3,2,1,0:T(8,128)(2,1)S(1)}, u32[]{:S(2)}, u32[]{:S(2)}) async-start(bf16[128,2,8,512]{3,2,1,0:T(8,128)(2,1)} %vertex_rows.7), calls=%async_computation.3 | async-start | bytes 4194304 | tf_op jit(solution)/shard_map/all_to_all | solution.py:152
  69.4 1.3 copy-start
  70.8 36.2 %all-to-all-start.2 = ((bf16[128,2,8,512]{3,2,1,0:T(8,128)(2,1)}), bf16[128,2,8,512]{3,2,1,0:T(8,128)(2,1)}, u32[]{:S(2)}, u32[]{:S(2)}) async-start(bf16[128,2,8,512]{3,2,1,0:T(8,128)(2,1)} %vertex_rows.6), calls=%async_computation.2 | async-start | bytes 4194304 | tf_op jit(solution)/shard_map/all_to_all | solution.py:152
  76.6 72.8 %all-gather.2.cloned.1.call-start = ((), (), s32[]{:S(2)}) async-start(), calls=%async_computation.5 | async-start | bytes 2621440 | tf_op jit(solution)/shard_map/all_gather | solution.py:142
  107.0 35.1 %all-to-all-start.1 = ((bf16[128,2,8,512]{3,2,1,0:T(8,128)(2,1)}), bf16[128,2,8,512]{3,2,1,0:T(8,128)(2,1)S(1)}, u32[]{:S(2)}, u32[]{:S(2)}) async-start(bf16[128,2,8,512]{3,2,1,0:T(8,128)(2,1)} %vertex_rows.5), calls=%async_computation.1 | async-start | bytes 4194304 | tf_op jit(solution)/shard_map/all_to_all | solution.py:152
  142.1 1.3 copy-start.1
  143.4 56.2 %all-to-all-start = ((bf16[128,2,8,512]{3,2,1,0:T(8,128)(2,1)}), bf16[128,2,8,512]{3,2,1,0:T(8,128)(2,1)}, u32[]{:S(2)}, u32[]{:S(2)}) async-start(bf16[128,2,8,512]{3,2,1,0:T(8,128)(2,1)} %vertex_rows.4), calls=%async_computation | async-start | bytes 4194304 | tf_op jit(solution)/shard_map/all_to_all | solution.py:152
Sparse Core Ops, SparseCore 0:
  79.1 38.0 all-gather.1

commit v2 on v1

v2 whole, which is shorter than its diff:
```python
import functools
import math

import jax
import jax.numpy as jnp
from jax import lax
from jax.experimental import pallas as pl
from jax.experimental.pallas import tpu as pltpu
from jax.sharding import PartitionSpec as P

G = 4096
AXES = ("kgrp", "band")
CHUNKS = 2
GC = 32 // CHUNKS
BLOCK = 512
BF, F32 = jnp.bfloat16, jnp.float32


def column(row):
    return jnp.transpose(jnp.broadcast_to(row, (128, 128)), (1, 0))


def pick(rows, row):
    here = lax.broadcasted_iota(jnp.int32, rows.shape, 0) == row
    return jnp.sum(jnp.where(here, rows, jnp.zeros_like(rows)), axis=0, keepdims=True)


def gather_kernel(own_ref, qtable_ref, map_ref, coul_ref, dens_ref, out_ref, onehot):
    row = lax.rem(qtable_ref[own_ref[0] + pl.program_id(0)], 8)
    lane = lax.broadcasted_iota(jnp.int32, (128, 128), 1)
    for b in range(BLOCK // 128):
        col = column(pick(map_ref[:, b * 128 : (b + 1) * 128], row))
        high = (col >> 7).astype(F32).astype(BF)
        low = jnp.where((col & 127) == lane, 1.0, 0.0).astype(BF)
        zero = jnp.zeros_like(low)
        for kb in range(G // 128):
            onehot[b * 128 : (b + 1) * 128, kb * 128 : (kb + 1) * 128] = jnp.where(
                high == jnp.asarray(kb, BF), low, zero
            )
    picked = lax.dot_general(
        onehot[...], dens_ref[0], (((1,), (1,)), ((), ())), preferred_element_type=F32
    )
    n = 128 // GC
    for b in range(BLOCK // 128):
        factor = column(pick(coul_ref[:, b * 128 : (b + 1) * 128], row))
        for l in range(4):
            scaled = picked[b * 128 : (b + 1) * 128, l * 128 : (l + 1) * 128] * factor
            out_ref[b * n : (b + 1) * n, 0, :, l * 128 : (l + 1) * 128] = scaled.reshape(n, GC, 128).astype(BF)


def gather(own, qtable, grid_map, coulomb, dens, chunk):
    steps = 128 * GC // BLOCK
    table = pl.BlockSpec((8, BLOCK), lambda r, i, own, qt: (qt[own[0] + r] // 8, chunk * steps + i))
    return pl.pallas_call(
        gather_kernel,
        grid_spec=pltpu.PrefetchScalarGridSpec(
            num_scalar_prefetch=2,
            grid=(2, steps),
            in_specs=[table, table, pl.BlockSpec((1, 512, G), lambda r, i, own, qt: (r, 0, 0))],
            out_specs=pl.BlockSpec((BLOCK // GC, 1, GC, 512), lambda r, i, own, qt: (i, r, 0, 0)),
            scratch_shapes=[pltpu.VMEM((BLOCK, G), BF)],
        ),
        out_shape=jax.ShapeDtypeStruct((128, 2, GC, 512), BF),
        compiler_params=pltpu.CompilerParams(vmem_limit_bytes=60 * 2**20),
        cost_estimate=pl.CostEstimate(flops=4 * 128 * GC * G * 512, bytes_accessed=10**7, transcendentals=0),
        name="vertex_rows",
    )(own, qtable, grid_map, coulomb, dens)


def ladder_kernel(first, last, own_ref, partner_ref, recv_ref, amp_ref, *refs):
    refs = list(refs)
    acc_in = None if first else refs.pop(0)
    out_ref, vert, mixed, wide = refs[:4]
    r = pl.program_id(0)

    @pl.when(r == 0)
    def _():
        for k in range(4):
            for r2 in range(2):
                for h in range(GC // 8):
                    for a4 in range(4):
                        wide[a4] = (
                            recv_ref[k, :, r2, h * 8 : (h + 1) * 8, a4 * 128 : (a4 + 1) * 128]
                            .astype(F32)
                            .reshape(256, 128)
                        )
                    for g in range(8):
                        for a4 in range(4):
                            vert[2 * k + r2, h * 8 + g, a4 * 32 : (a4 + 1) * 32, :] = wide[
                                a4, pl.ds(g, 32, stride=8), :
                            ].astype(BF)

    amp = jnp.concatenate([amp_ref[0, 0, ij] for ij in range(8)], axis=1)
    for g in range(GC):
        m = jnp.dot(vert[r, g], amp, preferred_element_type=F32).astype(BF)
        for ij in range(8):
            mixed[ij * 128 : (ij + 1) * 128, g * 128 : (g + 1) * 128] = m[:, ij * 128 : (ij + 1) * 128]
    w = vert[partner_ref[r]]
    right = jnp.concatenate([w[g] for g in range(GC)], axis=1)
    res = lax.dot_general(mixed[...], right, (((1,), (1,)), ((), ())), preferred_element_type=F32)
    if not first:
        res = res + acc_in[0]
    if last:
        total = refs[4]
        total[...] = res
        for s in range(32):
            out_ref[0, s, 0, :, :] = total[pl.ds(s, 32, stride=32), :].astype(BF)
    else:
        out_ref[0] = res


def piece(r, own):
    away = (r // 2) ^ (own // 2)
    return (away % 2) * 2 + away // 2


def ladder(own, partner, recv, amp, acc, last):
    ins = [
        pl.BlockSpec((4, 32, 2, GC, 512), lambda r, o, p: (0, 0, 0, 0, 0)),
        pl.BlockSpec((1, 1, 8, 128, 128), lambda r, o, p: (piece(r, o[0]), r % 2, 0, 0, 0)),
    ]
    args = [own, partner, recv.reshape(4, 32, 2, GC, 512), amp]
    if acc is not None:
        ins.append(pl.BlockSpec((1, 1024, 128), lambda r, o, p: (r, 0, 0)))
        args.append(acc)
    scratch = [
        pltpu.VMEM((8, GC, 128, 128), BF),
        pltpu.VMEM((1024, GC * 128), BF),
        pltpu.VMEM((4, 256, 128), F32),
    ]
    if last:
        out_spec = pl.BlockSpec((1, 32, 1, 32, 128), lambda r, o, p: (r // 2, 0, r % 2, 0, 0))
        out_shape = jax.ShapeDtypeStruct((4, 32, 2, 32, 128), BF)
        scratch.append(pltpu.VMEM((1024, 128), F32))
    else:
        out_spec = pl.BlockSpec((1, 1024, 128), lambda r, o, p: (r, 0, 0))
        out_shape = jax.ShapeDtypeStruct((8, 1024, 128), F32)
    return pl.pallas_call(
        functools.partial(ladder_kernel, acc is None, last),
        grid_spec=pltpu.PrefetchScalarGridSpec(
            num_scalar_prefetch=2, grid=(8,), in_specs=ins, out_specs=out_spec, scratch_shapes=scratch
        ),
        out_shape=out_shape,
        compiler_params=pltpu.CompilerParams(vmem_limit_bytes=60 * 2**20),
        cost_estimate=pl.CostEstimate(flops=4 * 64 * 128**3 * GC, bytes_accessed=12 * 10**6, transcendentals=0),
        name="ladder_sum",
    )(*args)


def swap(array, bit):
    return lax.ppermute(array, "kgrp", [(i, i ^ bit) for i in range(4)])


def shards(densities, amplitudes, partner, qtable, grid_map, coulomb):
    own = (lax.axis_index("kgrp") * 2).astype(jnp.int32).reshape(1)
    across = swap(amplitudes, 2)
    dens = densities.reshape(2, 512, G)
    received = []
    for q in range(CHUNKS):
        sent = gather(own, qtable, grid_map, coulomb, dens, q)
        if q == 0:
            sent, across = lax.optimization_barrier((sent, across))
            here = jnp.stack([amplitudes, across])
            amp = jnp.concatenate([here, swap(here, 1)])
        received.append(lax.all_to_all(sent, AXES, 0, 0, tiled=True))
    acc = None
    for q in range(CHUNKS):
        acc = ladder(own, partner, received[q], amp, acc, q == CHUNKS - 1)
    parts = lax.all_to_all(acc.reshape(128, 64, 128), AXES, 0, 0, tiled=True)
    total = jnp.sum(parts.astype(F32), axis=0) * (1.0 / math.sqrt(G))
    total = total.astype(BF).reshape(2, 8, 4, 4, 32)
    return jnp.transpose(total, (2, 0, 1, 4, 3)).reshape(4, 2, 8, 128)


def solution(mesh):
    in_specs = (P("kgrp", "band", None, None), P("kgrp", None, None, None), P(), P(), P(), P())
    out_specs = P("band", "kgrp", None, None)
    return jax.shard_map(shards, mesh=mesh, in_specs=in_specs, out_specs=out_specs, check_vma=False)
```

time: 268 us -> 215 us (0.80)
  between operations: 17.3 us -> 0.06 us
  Pallas kernels: 121 us -> 104 us
  local copies, waits for them, and re-layouts: 12 us -> 1.02 us
  starting transfers between devices: 27.5 us -> 18.6 us
  blocking collectives: 40 us -> 35.3 us
  waiting for transfers between devices: 49 us -> 53.6 us
    pallas_call x4 -> x2, Pallas kernels: 69.2 us -> 56 us  [ladder(): pl.pallas_call(functools.partial(ladder_kernel, acc is None, last), grid_...]
    all_to_all x4 -> x2, starting transfers between devices: 27.5 us -> 14.4 us  [shards(): received.append(lax.all_to_all(sent, AXES, 0, 0, tiled=True))]
    reshape x8 -> x0, local copies, waits for them, and re-layouts: 4.9 us -> none  [the longest x4 2.46 us: gather(): maps.reshape(2, steps, BLOCK // 128, 128)]
    all_to_all x1, blocking collectives: 40 us -> 35.3 us  [shards(): parts = lax.all_to_all(acc.reshape(128, 64, 128), AXES, 0, 0, tiled=True)]
    ppermute x0 -> x2, starting transfers between devices: none -> 4.23 us  [swap(): return lax.ppermute(array, 'kgrp', [(i, i ^ bit) for i in range(4)])]
    dynamic_slice x3 -> x0, local copies, waits for them, and re-layouts: 3.39 us -> none  [the longest x1 1.38 us: shards(): rows = [qtable[own + i] for i in range(2)]]
    pallas_call x4 -> x2, Pallas kernels: 51.4 us -> 48.1 us  [gather(): pl.pallas_call(gather_kernel, grid_spec=pltpu.PrefetchScalarGridSpec(num_...]
    all_to_all x4 -> x2, waiting for transfers between devices: 48.3 us -> 51 us  [shards(): received.append(lax.all_to_all(sent, AXES, 0, 0, tiled=True))]
  transfers between devices with their start and end apart: 5 -> 4, of which waited for: 3 -> 3; matrix products, arithmetic and copies ran while one was open for 1% -> 1% of each run, Pallas kernels for 33% -> 35%
where the time goes in v2:
time: 215 us
  Pallas kernels  104 us (48%)
  waiting for transfers between devices  53.6 us (25%)
  blocking collectives  35.3 us (16%)
  starting transfers between devices  18.6 us (9%)
    pallas_call x2, Pallas kernels, ladder(): pl.pallas_call(functools.partial(ladder_kernel, acc is None, last), grid_...  56 us
    all_to_all x2, waiting for transfers between devices, shards(): received.append(lax.all_to_all(sent, AXES, 0, 0, tiled=True))  51 us
    pallas_call x2, Pallas kernels, gather(): pl.pallas_call(gather_kernel, grid_spec=pltpu.PrefetchScalarGridSpec(num_...  48.1 us
    all_to_all x1, blocking collectives, shards(): parts = lax.all_to_all(acc.reshape(128, 64, 128), AXES, 0, 0, tiled=True)  35.3 us
    all_to_all x2, starting transfers between devices, shards(): received.append(lax.all_to_all(sent, AXES, 0, 0, tiled=True))  14.4 us
  transfers between devices with their start and end apart: 4, of which 3 were waited for; matrix products, arithmetic and copies ran while one was open for 1% of the time, Pallas kernels for 35%

profile of v2, /device:TPU:0, one launch (start us, length us, event | category | flops | bytes accessed | tf_op | source)
XLA Modules:
  0.0 214.8 jit_solution(10474243380375355337)
XLA Ops:
  0.0 4.0 %collective-permute-start = (bf16[2,8,128,128]{3,2,1,0:T(8,128)(2,1)}, bf16[2,8,128,128]{3,2,1,0:T(8,128)(2,1)S(1)}, u32[]{:S(2)}, u32[]{:S(2)}) collective-permute-start(bf16[2,8,128,128]{3,2,1,0:T(8,128)(2,1)} %param.7), channel_id=1, source_target_pairs={{0,64},{32,96},{64,0},{96,32},{1,65},{33,97},{65,1},{97,33},{2,66}... | collective-permute-start | bytes 1572872 | tf_op jit(solution)/shard_map/ppermute | solution.py:151
  4.0 24.1 %vertex_rows.3 = bf16[128,2,16,512]{3,2,1,0:T(8,128)(2,1)} custom-call(s32[1]{0:T(128)} %bitcast.own_ref, s32[8]{0:T(128)} %qtable_ref.3, s32[64,4096]{1,0:T(8,128)} %map_ref.3, f32[64,4096]{1,0:T(8,128)} %coul_ref.3, bf16[2,512,4096]{2,1,0:T(8,128)(2,1)} %bitcast.16), custom_call_target="tpu_custom_call" | custom-call | flops 17179869184 | bytes 10000000 | tf_op jit(solution)/shard_map/vertex_rows/pallas_call | solution.py:54
  28.0 0.0 collective-permute-done
  28.0 8.6 %all-to-all-start.1 = ((bf16[128,2,16,512]{3,2,1,0:T(8,128)(2,1)}), bf16[128,2,16,512]{3,2,1,0:T(8,128)(2,1)}, u32[]{:S(2)}, u32[]{:S(2)}) async-start(bf16[128,2,16,512]{3,2,1,0:T(8,128)(2,1)} %vertex_rows.3), calls=%async_computation.1 | async-start | bytes 8388608 | tf_op jit(solution)/shard_map/all_to_all | solution.py:165
  36.6 24.1 %vertex_rows.2 = bf16[128,2,16,512]{3,2,1,0:T(8,128)(2,1)} custom-call(s32[1]{0:T(128)} %bitcast.own_ref, s32[8]{0:T(128)} %qtable_ref.3, s32[64,4096]{1,0:T(8,128)} %map_ref.3, f32[64,4096]{1,0:T(8,128)} %coul_ref.3, bf16[2,512,4096]{2,1,0:T(8,128)(2,1)} %bitcast.17), custom_call_target="tpu_custom_call" | custom-call | flops 17179869184 | bytes 10000000 | tf_op jit(solution)/shard_map/vertex_rows/pallas_call | solution.py:54
  60.7 0.0 copy-start
  60.7 29.2 %all-to-all-done.1 = bf16[128,2,16,512]{3,2,1,0:T(8,128)(2,1)} async-done(((bf16[128,2,16,512]{3,2,1,0:T(8,128)(2,1)}), bf16[128,2,16,512]{3,2,1,0:T(8,128)(2,1)}, u32[]{:S(2)}, u32[]{:S(2)}) %all-to-all-start.1) | async-done | bytes 4194336 | tf_op jit(solution)/shard_map/all_to_all | solution.py:165
  89.8 5.8 %all-to-all-start = ((bf16[128,2,16,512]{3,2,1,0:T(8,128)(2,1)}), bf16[128,2,16,512]{3,2,1,0:T(8,128)(2,1)}, u32[]{:S(2)}, u32[]{:S(2)}) async-start(bf16[128,2,16,512]{3,2,1,0:T(8,128)(2,1)} %vertex_rows.2), calls=%async_computation | async-start | bytes 8388608 | tf_op jit(solution)/shard_map/all_to_all | solution.py:165
  95.7 0.0 copy-done
  95.7 0.1 pad_maximum_fusion.1
  95.8 0.3 collective-permute-start.1
  96.1 2.6 %collective-permute-done.1 = bf16[2,2,8,128,128]{4,3,2,1,0:T(8,128)(2,1)S(1)} collective-permute-done((bf16[2,2,8,128,128]{4,3,2,1,0:T(8,128)(2,1)S(1)}, bf16[2,2,8,128,128]{4,3,2,1,0:T(8,128)(2,1)S(1)}, u32[]{:S(2)}, u32[]{:S(2)}) %collective-permute-start.1) | collective-permute-done | bytes 1048608 | tf_op jit(solution)/shard_map/ppermute | solution.py:151
  98.7 1.5 pad_maximum_fusion.amp_ref
  100.3 26.9 %ladder_sum.2.refs_0_ = f32[8,1024,128]{2,1,0:T(8,128)} custom-call(s32[1]{0:T(128)} %bitcast.own_ref, s32[8]{0:T(128)} %partner_ref.3, bf16[4,32,2,16,512]{4,3,2,1,0:T(8,128)(2,1)} %bitcast.5.recv_ref, bf16[4,2,8,128,128]{4,3,2,1,0:T(8,128)(2,1)} %pad_maximum_fusion.amp_ref), custom_call_target="tpu_custom_call" | custom-call | flops 8589934592 | bytes 12000000 | tf_op jit(solution)/shard_map/ladder_sum/pallas_call | solution.py:138
  127.1 21.8 %all-to-all-done = bf16[128,2,16,512]{3,2,1,0:T(8,128)(2,1)} async-done(((bf16[128,2,16,512]{3,2,1,0:T(8,128)(2,1)}), bf16[128,2,16,512]{3,2,1,0:T(8,128)(2,1)}, u32[]{:S(2)}, u32[]{:S(2)}) %all-to-all-start) | async-done | bytes 4194336 | tf_op jit(solution)/shard_map/all_to_all | solution.py:165
  148.9 29.2 %ladder_sum.3 = bf16[4,32,2,32,128]{4,3,2,1,0:T(8,128)(2,1)} custom-call(s32[1]{0:T(128)} %bitcast.own_ref, s32[8]{0:T(128)} %partner_ref.3, bf16[4,32,2,16,512]{4,3,2,1,0:T(8,128)(2,1)} %bitcast.2.recv_ref, bf16[4,2,8,128,128]{4,3,2,1,0:T(8,128)(2,1)} %pad_maximum_fusion.amp_ref, f32[8,1024,128]{2,1,0:T(8,128)} %ladder_sum.2.refs_0_), custom_call_target="tpu_custom_call" | custom-call | flops 8589934592 | bytes 12000000 | tf_op jit(solution)/shard_map/ladder_sum/pallas_call | solution.py:138
  178.1 35.3 %all_to_all.15 = bf16[128,64,128]{2,1,0:T(8,128)(2,1)S(1)} all-to-all(bf16[128,64,128]{2,1,0:T(8,128)(2,1)} %bitcast.9), channel_id=1, replica_groups=mesh['kgrp'=4,'band'=32] {'kgrp','band'}, dimensions={0} | all-to-all | bytes 4194304 | tf_op jit(solution)/shard_map/all_to_all | solution.py:169
  213.4 0.4 convert_reduce_fusion
  213.8 0.1 convert_element_type.12
  213.9 0.2 copy.7
  214.1 0.7 copy.8
  (1 shorter events, 0.0 us)
Async XLA Ops:
  0.0 28.0 %collective-permute-start = (bf16[2,8,128,128]{3,2,1,0:T(8,128)(2,1)}, bf16[2,8,128,128]{3,2,1,0:T(8,128)(2,1)S(1)}, u32[]{:S(2)}, u32[]{:S(2)}) collective-permute-start(bf16[2,8,128,128]{3,2,1,0:T(8,128)(2,1)} %param.7), channel_id=1, source_target_pairs={{0,64},{32,96},{64,0},{96,32},{1,65},{33,97},{65,1},{97,33},{2,66}... | collective-permute-start | bytes 1572872 | tf_op jit(solution)/shard_map/ppermute | solution.py:151
  28.0 61.8 %all-to-all-start.1 = ((bf16[128,2,16,512]{3,2,1,0:T(8,128)(2,1)}), bf16[128,2,16,512]{3,2,1,0:T(8,128)(2,1)}, u32[]{:S(2)}, u32[]{:S(2)}) async-start(bf16[128,2,16,512]{3,2,1,0:T(8,128)(2,1)} %vertex_rows.3), calls=%async_computation.1 | async-start | bytes 8388608 | tf_op jit(solution)/shard_map/all_to_all | solution.py:165
  60.7 35.0 %copy-start = (bf16[2,8,128,128]{3,2,1,0:T(8,128)(2,1)S(1)}, bf16[2,8,128,128]{3,2,1,0:T(8,128)(2,1)}, u32[]{:S(2)}) copy-start(bf16[2,8,128,128]{3,2,1,0:T(8,128)(2,1)} %param.7) | copy-start | bytes 1572868
  89.8 59.1 %all-to-all-start = ((bf16[128,2,16,512]{3,2,1,0:T(8,128)(2,1)}), bf16[128,2,16,512]{3,2,1,0:T(8,128)(2,1)}, u32[]{:S(2)}, u32[]{:S(2)}) async-start(bf16[128,2,16,512]{3,2,1,0:T(8,128)(2,1)} %vertex_rows.2), calls=%async_computation | async-start | bytes 8388608 | tf_op jit(solution)/shard_map/all_to_all | solution.py:165
  95.8 2.9 %collective-permute-start.1 = (bf16[2,2,8,128,128]{4,3,2,1,0:T(8,128)(2,1)S(1)}, bf16[2,2,8,128,128]{4,3,2,1,0:T(8,128)(2,1)S(1)}, u32[]{:S(2)}, u32[]{:S(2)}) collective-permute-start(bf16[2,2,8,128,128]{4,3,2,1,0:T(8,128)(2,1)S(1)} %pad_maximum_fusion.1), channel_id=1, source_target_pairs={{0,32},{32,0},{64,96},{96,64},{1,33},{33,1},{65,97},{97,65},{2,34}... | collective-permute-start | bytes 3145736 | tf_op jit(solution)/shard_map/ppermute | solution.py:151

commit v3 on v0

v3 whole, which is shorter than its diff:
```python
import functools
import math

import jax
import jax.numpy as jnp
from jax import lax
from jax.experimental import pallas as pl
from jax.experimental.pallas import tpu as pltpu
from jax.sharding import PartitionSpec as P

G = 4096
AXES = ("kgrp", "band")
SIZES = (20, 12)
BF, F32 = jnp.bfloat16, jnp.float32


def pick(rows, row):
    here = lax.broadcasted_iota(jnp.int32, rows.shape, 0) == row
    return jnp.sum(jnp.where(here, rows, jnp.zeros_like(rows)), axis=0, keepdims=True)


def gather_kernel(gc, start, own_ref, qtable_ref, map_ref, dens_ref, out_ref, table, place_v, place_s, sem):
    row = lax.rem(qtable_ref[own_ref[0] + pl.program_id(0)], 8)
    for b in range(gc):
        p = pick(map_ref[:, start + b * 128 : start + (b + 1) * 128], row)
        place_v[b : b + 1, :] = ((p & 1) << 14) + ((p >> 1) << 3)
    copy = pltpu.make_async_copy(place_v, place_s, sem)
    copy.start()
    eye = lax.broadcasted_iota(jnp.int32, (256, 256), 0) == lax.broadcasted_iota(jnp.int32, (256, 256), 1)
    eye = jnp.where(eye, 1.0, 0.0).astype(BF)
    for i in range(G // 256):
        turned = lax.dot_general(
            eye, dens_ref[0, :, i * 256 : (i + 1) * 256], (((1,), (1,)), ((), ())), preferred_element_type=F32
        )
        for a in range(4):
            table[pl.ds(i * 1024 + a, 256, stride=4), :] = turned[:, a * 128 : (a + 1) * 128]
        for j in range(128):
            at = i * 1024 + j * 8
            table[4 * G + at : 4 * G + at + 8, :] = pltpu.roll(table[at : at + 8, :], 4, 0)
    copy.wait()
    low = lax.broadcasted_iota(jnp.int32, (8, 128), 0) < 4
    step = math.lcm(128, gc)

    def body(it, _):
        for quad in range(step // 4):
            pairs = []
            for h in range(2):
                at = quad * 4 + h * 2
                block = it * (step // 128) + at // 128
                first = place_s[block, at % 128]
                second = place_s[block, at % 128 + 1] ^ (1 << 14)
                pairs.append(
                    jnp.where(
                        low,
                        table[pl.ds(pl.multiple_of(first, 8), 8), :],
                        table[pl.ds(pl.multiple_of(second, 8), 8), :],
                    )
                )
            device, w = divmod(quad * 4, gc)
            out_ref[it * (step // gc) + device, 0, 4 * w : 4 * w + 16, :] = jnp.concatenate(pairs, axis=0).astype(BF)
        return 0

    lax.fori_loop(0, 128 * gc // step, body, 0)


def gather(own, qtable, grid_map, dens, gc, start):
    return pl.pallas_call(
        functools.partial(gather_kernel, gc, start),
        grid_spec=pltpu.PrefetchScalarGridSpec(
            num_scalar_prefetch=2,
            grid=(2,),
            in_specs=[
                pl.BlockSpec((8, G), lambda r, own, qt: (qt[own[0] + r] // 8, 0)),
                pl.BlockSpec((1, 512, G), lambda r, own, qt: (r, 0, 0)),
            ],
            out_specs=pl.BlockSpec((128, 1, 4 * gc, 128), lambda r, own, qt: (0, r, 0, 0)),
            scratch_shapes=[
                pltpu.VMEM((8 * G, 128), F32),
                pltpu.VMEM((gc, 128), jnp.int32),
                pltpu.SMEM((gc, 128), jnp.int32),
                pltpu.SemaphoreType.DMA,
            ],
        ),
        out_shape=jax.ShapeDtypeStruct((128, 2, 4 * gc, 128), BF),
        compiler_params=pltpu.CompilerParams(vmem_limit_bytes=60 * 2**20),
        cost_estimate=pl.CostEstimate(flops=2 * 10**10, bytes_accessed=10**7, transcendentals=0),
        name="vertex_rows",
    )(own, qtable, grid_map, dens)


def ladder_kernel(gc, first, last, own_ref, partner_ref, qtable_ref, coul_ref, recv_ref, amp_ref, *refs):
    refs = list(refs)
    acc_in = None if first else refs.pop(0)
    out_ref, vert, mixed, wide = refs[:4]
    k = pl.program_id(0)

    @pl.when(k == 0)
    def _():
        for k in range(4):
            for r2 in range(2):
                part = wide.at[r2]
                for s in range(32):
                    part[s * (4 * gc + 8) : s * (4 * gc + 8) + 4 * gc, :] = recv_ref[k, s, r2].astype(F32)
                base = qtable_ref[2 * k + r2] * gc
                for g in range(gc):
                    factor = coul_ref[base + g]
                    for a4 in range(4):
                        rows = part[pl.ds(4 * g + a4, 32, stride=4 * gc + 8), :]
                        vert[2 * k + r2, g, a4 * 32 : (a4 + 1) * 32, :] = (rows * factor).astype(BF)

    for i in range(2):
        amp = jnp.concatenate([amp_ref[0, i, ij] for ij in range(8)], axis=1)
        for g in range(gc):
            m = jnp.dot(vert[2 * k + i, g], amp, preferred_element_type=F32).astype(BF)
            for ij in range(8):
                mixed[i, ij * 128 : (ij + 1) * 128, g * 128 : (g + 1) * 128] = m[:, ij * 128 : (ij + 1) * 128]
    for i in range(2):
        other = partner_ref[2 * k + i]
        right = jnp.concatenate([vert[other, g] for g in range(gc)], axis=1)
        res = lax.dot_general(mixed[i], right, (((1,), (1,)), ((), ())), preferred_element_type=F32)
        if not first:
            res = res + acc_in[i]
        if last:
            total = refs[4].at[i]
            total[...] = res
            for s in range(32):
                out_ref[0, s, i, :, :] = total[pl.ds(s, 32, stride=32), :].astype(BF)
        else:
            out_ref[i] = res


def piece(k, own):
    away = k ^ (own // 2)
    return (away % 2) * 2 + away // 2


def ladder(own, partner, qtable, coul, recv, amp, acc, last, gc):
    ins = [
        pl.BlockSpec((4, 32, 2, 4 * gc, 128), lambda k, *_: (0, 0, 0, 0, 0)),
        pl.BlockSpec((1, 2, 8, 128, 128), lambda k, o, *_: (piece(k, o[0]), 0, 0, 0, 0)),
    ]
    args = [own, partner, qtable, coul, recv.reshape(4, 32, 2, 4 * gc, 128), amp]
    if acc is not None:
        ins.append(pl.BlockSpec((2, 1024, 128), lambda k, *_: (k, 0, 0)))
        args.append(acc)
    scratch = [
        pltpu.VMEM((8, gc, 128, 128), BF),
        pltpu.VMEM((2, 1024, gc * 128), BF),
        pltpu.VMEM((2, 32 * (4 * gc + 8), 128), F32),
    ]
    if last:
        out_spec = pl.BlockSpec((1, 32, 2, 32, 128), lambda k, *_: (k, 0, 0, 0, 0))
        out_shape = jax.ShapeDtypeStruct((4, 32, 2, 32, 128), BF)
        scratch.append(pltpu.VMEM((2, 1024, 128), F32))
    else:
        out_spec = pl.BlockSpec((2, 1024, 128), lambda k, *_: (k, 0, 0))
        out_shape = jax.ShapeDtypeStruct((8, 1024, 128), F32)
    return pl.pallas_call(
        functools.partial(ladder_kernel, gc, acc is None, last),
        grid_spec=pltpu.PrefetchScalarGridSpec(
            num_scalar_prefetch=4, grid=(4,), in_specs=ins, out_specs=out_spec, scratch_shapes=scratch
        ),
        out_shape=out_shape,
        compiler_params=pltpu.CompilerParams(vmem_limit_bytes=60 * 2**20),
        cost_estimate=pl.CostEstimate(flops=4 * 64 * 128**3 * gc, bytes_accessed=12 * 10**6, transcendentals=0),
        name="ladder_sum",
    )(*args)


def swap(array, bit):
    return lax.ppermute(array, "kgrp", [(i, i ^ bit) for i in range(4)])


def shards(densities, amplitudes, partner, qtable, grid_map, coulomb):
    own = (lax.axis_index("kgrp") * 2).astype(jnp.int32).reshape(1)
    across = swap(amplitudes, 2)
    dens = densities.reshape(2, 512, G)
    device = lax.axis_index(AXES)
    received, couls, start = [], [], 0
    for q, gc in enumerate(SIZES):
        sent = gather(own, qtable, grid_map, dens, gc, start)
        if q == 0:
            sent, across = lax.optimization_barrier((sent, across))
            here = jnp.stack([amplitudes, across])
            amp = jnp.concatenate([here, swap(here, 1)])
        received.append(lax.all_to_all(sent, AXES, 0, 0, tiled=True))
        couls.append(lax.dynamic_slice(coulomb, (0, start + device * gc), (64, gc)).reshape(-1))
        start += 128 * gc
    acc = None
    for q, gc in enumerate(SIZES):
        acc = ladder(own, partner, qtable, couls[q], received[q], amp, acc, q == len(SIZES) - 1, gc)
    parts = lax.all_to_all(acc.reshape(128, 64, 128), AXES, 0, 0, tiled=True)
    total = jnp.sum(parts.astype(F32), axis=0) * (1.0 / math.sqrt(G))
    total = total.astype(BF).reshape(2, 8, 4, 4, 32)
    return jnp.transpose(total, (2, 0, 1, 4, 3)).reshape(4, 2, 8, 128)


def solution(mesh):
    in_specs = (P("kgrp", "band", None, None), P("kgrp", None, None, None), P(), P(), P(), P())
    out_specs = P("band", "kgrp", None, None)
    return jax.shard_map(shards, mesh=mesh, in_specs=in_specs, out_specs=out_specs, check_vma=False)
```

time: 802 us -> 199 us (0.25)
  waiting for transfers between devices: 344 us -> 60.4 us
  local copies, waits for them, and re-layouts: 184 us -> 2.58 us
  matrix products: 123 us -> 0 us
  Pallas kernels: 0 us -> 78.5 us
  blocking collectives: 104 us -> 35.3 us
  other arithmetic: 31.3 us -> 3.2 us
  starting transfers between devices: 0.22 us -> 18.4 us
  between operations: 13.5 us -> 0.11 us
    all_gather x1 -> x0, waiting for transfers between devices: 183 us -> none  [shards(): everything = lax.all_gather(vertex, 'kgrp', axis=0, tiled=True)]
    reduce_scatter x1 -> x0, waiting for transfers between devices: 160 us -> none  [shards(): lax.psum_scatter(jnp.transpose(stacked, (2, 0, 1, 3)), 'band', scatter_di...]
    dot_general x32 -> x0, matrix products: 123 us -> none  [the longest x16 65.9 us: one_slab(): jnp.einsum('adg,bdg->ab', mixed, right_pair, preferred_element_type=jnp.f...]
    gather x9 -> x0, local copies, waits for them, and re-layouts: 88.3 us -> none  [the longest x1 71.6 us: shards(): jnp.take(dens_block, grid_rows, axis=2)]
    pallas_call x0 -> x4, Pallas kernels: none -> 78.5 us  [the longest x2 51.7 us: ladder(): pl.pallas_call(functools.partial(ladder_kernel, gc, acc is None, last), g...]
    all_to_all x1, blocking collectives: 104 us -> 35.3 us  [shards(): parts = lax.all_to_all(acc.reshape(128, 64, 128), AXES, 0, 0, tiled=True)]
    all_to_all x0 -> x2, waiting for transfers between devices: none -> 59.2 us  [shards(): received.append(lax.all_to_all(sent, AXES, 0, 0, tiled=True))]
    dynamic_update_slice x16 -> x0, local copies, waits for them, and re-layouts: 23 us -> none  [shards(): pieces.append(lax.map(one_slab, amplitudes[pair_index]))]
  transfers between devices with their start and end apart: 2 -> 4, of which waited for: 2 -> 3; matrix products, arithmetic and copies ran while one was open for 3% -> 2% of each run, Pallas kernels for 0% -> 28%
where the time goes in v3:
time: 199 us; the launch traced here: 198 us
  Pallas kernels  78.5 us (39%)
  waiting for transfers between devices  60.4 us (30%)
  blocking collectives  35.3 us (18%)
  starting transfers between devices  18.4 us (9%)
  other arithmetic  3.2 us (2%)
  local copies, waits for them, and re-layouts  2.58 us (1%)
    all_to_all x2, waiting for transfers between devices, shards(): received.append(lax.all_to_all(sent, AXES, 0, 0, tiled=True))  59.2 us
    pallas_call x2, Pallas kernels, ladder(): pl.pallas_call(functools.partial(ladder_kernel, gc, acc is None, last), g...  51.7 us
    all_to_all x1, blocking collectives, shards(): parts = lax.all_to_all(acc.reshape(128, 64, 128), AXES, 0, 0, tiled=True)  35.3 us
    pallas_call x2, Pallas kernels, gather(): pl.pallas_call(functools.partial(gather_kernel, gc, start), grid_spec=plt...  26.8 us
    all_to_all x2, starting transfers between devices, shards(): received.append(lax.all_to_all(sent, AXES, 0, 0, tiled=True))  14.3 us
    ppermute x2, starting transfers between devices, swap(): return lax.ppermute(array, 'kgrp', [(i, i ^ bit) for i in range(4)])  4.05 us
  transfers between devices with their start and end apart: 4, of which 3 were waited for; matrix products, arithmetic and copies ran while one was open for 2% of the time, Pallas kernels for 28%

profile of v3, /device:TPU:0, one launch (start us, length us, event | category | flops | bytes accessed | tf_op | source)
XLA Modules:
  0.0 198.4 jit_solution(1676350691575515382)
XLA Ops:
  0.0 0.0 copy-start
  0.0 4.0 %collective-permute-start = (bf16[2,8,128,128]{3,2,1,0:T(8,128)(2,1)}, bf16[2,8,128,128]{3,2,1,0:T(8,128)(2,1)S(1)}, u32[]{:S(2)}, u32[]{:S(2)}) collective-permute-start(bf16[2,8,128,128]{3,2,1,0:T(8,128)(2,1)} %param.7), channel_id=1, source_target_pairs={{0,64},{32,96},{64,0},{96,32},{1,65},{33,97},{65,1},{97,33},{2,66}... | collective-permute-start | bytes 1572872 | tf_op jit(solution)/shard_map/ppermute | solution.py:171
  4.0 14.6 %vertex_rows.3 = bf16[128,2,80,128]{3,2,1,0:T(8,128)(2,1)} custom-call(s32[1]{0:T(128)} %bitcast.own_ref, s32[8]{0:T(128)} %qtable_ref.7, s32[64,4096]{1,0:T(8,128)} %map_ref.3, bf16[2,512,4096]{2,1,0:T(8,128)(2,1)} %bitcast.16), custom_call_target="tpu_custom_call" | custom-call | flops 20000000000 | bytes 10000000 | tf_op jit(solution)/shard_map/vertex_rows/pallas_call | solution.py:67
  18.6 0.0 collective-permute-done
  18.6 8.5 %all-to-all-start.1 = ((bf16[128,2,80,128]{3,2,1,0:T(8,128)(2,1)}), bf16[128,2,80,128]{3,2,1,0:T(8,128)(2,1)}, u32[]{:S(2)}, u32[]{:S(2)}) async-start(bf16[128,2,80,128]{3,2,1,0:T(8,128)(2,1)} %vertex_rows.3), calls=%async_computation.1 | async-start | bytes 10485760 | tf_op jit(solution)/shard_map/all_to_all | solution.py:186
  27.1 12.2 %vertex_rows.2 = bf16[128,2,48,128]{3,2,1,0:T(8,128)(2,1)} custom-call(s32[1]{0:T(128)} %bitcast.own_ref, s32[8]{0:T(128)} %qtable_ref.7, s32[64,4096]{1,0:T(8,128)} %map_ref.3, bf16[2,512,4096]{2,1,0:T(8,128)(2,1)} %bitcast.17), custom_call_target="tpu_custom_call" | custom-call | flops 20000000000 | bytes 10000000 | tf_op jit(solution)/shard_map/vertex_rows/pallas_call | solution.py:67
  39.3 0.0 copy-start.1
  39.3 52.8 %all-to-all-done.1 = bf16[128,2,80,128]{3,2,1,0:T(8,128)(2,1)} async-done(((bf16[128,2,80,128]{3,2,1,0:T(8,128)(2,1)}), bf16[128,2,80,128]{3,2,1,0:T(8,128)(2,1)}, u32[]{:S(2)}, u32[]{:S(2)}) %all-to-all-start.1) | async-done | bytes 5242912 | tf_op jit(solution)/shard_map/all_to_all | solution.py:186
  92.1 5.8 %all-to-all-start = ((bf16[128,2,48,128]{3,2,1,0:T(8,128)(2,1)}), bf16[128,2,48,128]{3,2,1,0:T(8,128)(2,1)}, u32[]{:S(2)}, u32[]{:S(2)}) async-start(bf16[128,2,48,128]{3,2,1,0:T(8,128)(2,1)} %vertex_rows.2), calls=%async_computation | async-start | bytes 6291456 | tf_op jit(solution)/shard_map/all_to_all | solution.py:186
  97.9 0.0 copy-done.1
  97.9 0.1 pad_maximum_fusion.1
  98.0 0.1 collective-permute-start.1
  98.1 0.0 copy-done
  98.1 0.1 constant_dynamic-slice_fusion
  98.2 0.7 reshape.33.coul_ref
  98.9 0.1 constant_dynamic-slice_fusion.1
  99.0 0.7 reshape.30.coul_ref
  99.7 1.2 collective-permute-done.1
  100.9 2.7 %pad_maximum_fusion.amp_ref = bf16[4,2,8,128,128]{4,3,2,1,0:T(8,128)(2,1)} fusion(bf16[2,2,8,128,128]{4,3,2,1,0:T(8,128)(2,1)} %collective-permute-done.1, bf16[1,2,8,128,128]{4,3,2,1,0:T(8,128)(2,1)S(1)} %bitcast.13, bf16[1,2,8,128,128]{4,3,2,1,0:T(8,128)(2,1)S(1)} %bitcast.11), kind=kLoop, calls=%fused_computation.1 | loop fusion | flops 2097152 | bytes 4194304 | tf_op jit(solution)/shard_map/concatenate | solution.py:185
  103.6 29.4 %ladder_sum.2.refs_0_ = f32[8,1024,128]{2,1,0:T(8,128)} custom-call(s32[1]{0:T(128)} %bitcast.own_ref, s32[8]{0:T(128)} %partner_ref.3, s32[8]{0:T(128)} %qtable_ref.7, f32[1280]{0:T(1024)} %reshape.33.coul_ref, bf16[4,32,2,80,128]{4,3,2,1,0:T(8,128)(2,1)} %bitcast.5.recv_ref, bf16[4,2,8,128,128]{4,3,2,1,0:T(8,128)(2,1)} %pad_maximum_fusion.amp_ref), custom_call_target="tpu_custom_call" | custom-call | flops 10737418240 | bytes 12000000 | tf_op jit(solution)/shard_map/ladder_sum/pallas_call | solution.py:158
  133.0 6.4 %all-to-all-done = bf16[128,2,48,128]{3,2,1,0:T(8,128)(2,1)} async-done(((bf16[128,2,48,128]{3,2,1,0:T(8,128)(2,1)}), bf16[128,2,48,128]{3,2,1,0:T(8,128)(2,1)}, u32[]{:S(2)}, u32[]{:S(2)}) %all-to-all-start) | async-done | bytes 3145760 | tf_op jit(solution)/shard_map/all_to_all | solution.py:186
  139.4 22.2 %ladder_sum.3 = bf16[4,32,2,32,128]{4,3,2,1,0:T(8,128)(2,1)} custom-call(s32[1]{0:T(128)} %bitcast.own_ref, s32[8]{0:T(128)} %partner_ref.3, s32[8]{0:T(128)} %qtable_ref.7, f32[768]{0:T(1024)} %reshape.30.coul_ref, bf16[4,32,2,48,128]{4,3,2,1,0:T(8,128)(2,1)} %bitcast.2.recv_ref, bf16[4,2,8,128,128]{4,3,2,1,0:T(8,128)(2,1)} %pad_maximum_fusion.amp_ref, ...), custom_call_target="tpu_custom_call" | custom-call | flops 6442450944 | bytes 12000000 | tf_op jit(solution)/shard_map/ladder_sum/pallas_call | solution.py:158
  161.7 35.3 %all_to_all.15 = bf16[128,64,128]{2,1,0:T(8,128)(2,1)S(1)} all-to-all(bf16[128,64,128]{2,1,0:T(8,128)(2,1)} %bitcast.9), channel_id=1, replica_groups=mesh['kgrp'=4,'band'=32] {'kgrp','band'}, dimensions={0} | all-to-all | bytes 4194304 | tf_op jit(solution)/shard_map/all_to_all | solution.py:192
  197.0 0.4 convert_reduce_fusion
  197.4 0.1 convert_element_type.12
  197.5 0.2 copy.7
  197.7 0.7 copy.8
  (1 shorter events, 0.0 us)
Async XLA Ops:
  0.0 98.1 %copy-start = (f32[64,4096]{1,0:T(8,128)S(1)}, f32[64,4096]{1,0:T(8,128)}, u32[]{:S(2)}) copy-start(f32[64,4096]{1,0:T(8,128)} %param.11) | copy-start | bytes 3145732
  0.0 18.6 %collective-permute-start = (bf16[2,8,128,128]{3,2,1,0:T(8,128)(2,1)}, bf16[2,8,128,128]{3,2,1,0:T(8,128)(2,1)S(1)}, u32[]{:S(2)}, u32[]{:S(2)}) collective-permute-start(bf16[2,8,128,128]{3,2,1,0:T(8,128)(2,1)} %param.7), channel_id=1, source_target_pairs={{0,64},{32,96},{64,0},{96,32},{1,65},{33,97},{65,1},{97,33},{2,66}... | collective-permute-start | bytes 1572872 | tf_op jit(solution)/shard_map/ppermute | solution.py:171
  18.6 73.5 %all-to-all-start.1 = ((bf16[128,2,80,128]{3,2,1,0:T(8,128)(2,1)}), bf16[128,2,80,128]{3,2,1,0:T(8,128)(2,1)}, u32[]{:S(2)}, u32[]{:S(2)}) async-start(bf16[128,2,80,128]{3,2,1,0:T(8,128)(2,1)} %vertex_rows.3), calls=%async_computation.1 | async-start | bytes 10485760 | tf_op jit(solution)/shard_map/all_to_all | solution.py:186
  39.3 58.6 %copy-start.1 = (bf16[2,8,128,128]{3,2,1,0:T(8,128)(2,1)S(1)}, bf16[2,8,128,128]{3,2,1,0:T(8,128)(2,1)}, u32[]{:S(2)}) copy-start(bf16[2,8,128,128]{3,2,1,0:T(8,128)(2,1)} %param.7) | copy-start | bytes 1572868
  92.1 47.3 %all-to-all-start = ((bf16[128,2,48,128]{3,2,1,0:T(8,128)(2,1)}), bf16[128,2,48,128]{3,2,1,0:T(8,128)(2,1)}, u32[]{:S(2)}, u32[]{:S(2)}) async-start(bf16[128,2,48,128]{3,2,1,0:T(8,128)(2,1)} %vertex_rows.2), calls=%async_computation | async-start | bytes 6291456 | tf_op jit(solution)/shard_map/all_to_all | solution.py:186
  98.0 2.9 %collective-permute-start.1 = (bf16[2,2,8,128,128]{4,3,2,1,0:T(8,128)(2,1)S(1)}, bf16[2,2,8,128,128]{4,3,2,1,0:T(8,128)(2,1)}, u32[]{:S(2)}, u32[]{:S(2)}) collective-permute-start(bf16[2,2,8,128,128]{4,3,2,1,0:T(8,128)(2,1)S(1)} %pad_maximum_fusion.1), channel_id=1, source_target_pairs={{0,32},{32,0},{64,96},{96,64},{1,33},{33,1},{65,97},{97,65},{2,34}... | collective-permute-start | bytes 3145736 | tf_op jit(solution)/shard_map/ppermute | solution.py:171

commit v4 on v3

--- a/solution.py
+++ b/solution.py
@@ -6,10 +6,12 @@
 from jax import lax
 from jax.experimental import pallas as pl
 from jax.experimental.pallas import tpu as pltpu
+from jax.sharding import Mesh
 from jax.sharding import PartitionSpec as P
 
 G = 4096
-AXES = ("kgrp", "band")
+KGRP = ("zhi", "core")
+AXES = KGRP + ("band",)
 SIZES = (20, 12)
 BF, F32 = jnp.bfloat16, jnp.float32
 
@@ -91,19 +93,21 @@
 def ladder_kernel(gc, first, last, own_ref, partner_ref, qtable_ref, coul_ref, recv_ref, amp_ref, *refs):
     refs = list(refs)
     acc_in = None if first else refs.pop(0)
-    out_ref, vert, mixed, wide = refs[:4]
-    k = pl.program_id(0)
-
-    @pl.when(k == 0)
+    outs = [refs.pop(0) for _ in range(1 + last)]
+    vert, mixed, wide = refs[:3]
+    t = pl.program_id(0)
+    k = turn(t, own_ref[0], last)
+
+    @pl.when(t == 0)
     def _():
         for k in range(4):
             for r2 in range(2):
                 part = wide.at[r2]
                 for s in range(32):
                     part[s * (4 * gc + 8) : s * (4 * gc + 8) + 4 * gc, :] = recv_ref[k, s, r2].astype(F32)
-                base = qtable_ref[2 * k + r2] * gc
+                q = qtable_ref[2 * k + r2]
                 for g in range(gc):
-                    factor = coul_ref[base + g]
+                    factor = coul_ref[q, g]
                     for a4 in range(4):
                         rows = part[pl.ds(4 * g + a4, 32, stride=4 * gc + 8), :]
                         vert[2 * k + r2, g, a4 * 32 : (a4 + 1) * 32, :] = (rows * factor).astype(BF)
@@ -121,12 +125,22 @@
         if not first:
             res = res + acc_in[i]
         if last:
-            total = refs[4].at[i]
-            total[...] = res
-            for s in range(32):
-                out_ref[0, s, i, :, :] = total[pl.ds(s, 32, stride=32), :].astype(BF)
+            for n in range(32):
+                refs[3][i, n * 40 : n * 40 + 32, :] = res[n * 32 : (n + 1) * 32]
         else:
-            out_ref[i] = res
+            outs[0][i] = res
+    if last:
+        for half, out_ref in enumerate(outs):
+
+            @pl.when(t // 2 == half)
+            def _():
+                for i in range(2):
+                    for s in range(32):
+                        out_ref[0, s, i, :, :] = refs[3][i, pl.ds(s, 32, stride=40), :].astype(BF)
+
+
+def turn(t, own, last):
+    return 2 * (t % 2) + (((own // 2) % 2) ^ (1 - t // 2)) if last else t
 
 
 def piece(k, own):
@@ -137,21 +151,24 @@
 def ladder(own, partner, qtable, coul, recv, amp, acc, last, gc):
     ins = [
         pl.BlockSpec((4, 32, 2, 4 * gc, 128), lambda k, *_: (0, 0, 0, 0, 0)),
-        pl.BlockSpec((1, 2, 8, 128, 128), lambda k, o, *_: (piece(k, o[0]), 0, 0, 0, 0)),
+        pl.BlockSpec((1, 2, 8, 128, 128), lambda t, o, *_: (piece(turn(t, o[0], last), o[0]), 0, 0, 0, 0)),
     ]
     args = [own, partner, qtable, coul, recv.reshape(4, 32, 2, 4 * gc, 128), amp]
     if acc is not None:
-        ins.append(pl.BlockSpec((2, 1024, 128), lambda k, *_: (k, 0, 0)))
+        ins.append(pl.BlockSpec((2, 1024, 128), lambda t, o, *_: (turn(t, o[0], last), 0, 0)))
         args.append(acc)
     scratch = [
         pltpu.VMEM((8, gc, 128, 128), BF),
         pltpu.VMEM((2, 1024, gc * 128), BF),
-        pltpu.VMEM((2, 32 * (4 * gc + 8), 128), F32),
+        pltpu.VMEM((2, 33 * (4 * gc + 8), 128), F32),
     ]
     if last:
-        out_spec = pl.BlockSpec((1, 32, 2, 32, 128), lambda k, *_: (k, 0, 0, 0, 0))
-        out_shape = jax.ShapeDtypeStruct((4, 32, 2, 32, 128), BF)
-        scratch.append(pltpu.VMEM((2, 1024, 128), F32))
+        out_spec = [
+            pl.BlockSpec((1, 32, 2, 32, 128), lambda t, *_: (jnp.minimum(t, 1), 0, 0, 0, 0)),
+            pl.BlockSpec((1, 32, 2, 32, 128), lambda t, *_: (jnp.maximum(t - 2, 0), 0, 0, 0, 0)),
+        ]
+        out_shape = [jax.ShapeDtypeStruct((2, 32, 2, 32, 128), BF)] * 2
+        scratch.append(pltpu.VMEM((2, 33 * 40, 128), F32))
     else:
         out_spec = pl.BlockSpec((2, 1024, 128), lambda k, *_: (k, 0, 0))
         out_shape = jax.ShapeDtypeStruct((8, 1024, 128), F32)
@@ -167,13 +184,13 @@
     )(*args)
 
 
-def swap(array, bit):
-    return lax.ppermute(array, "kgrp", [(i, i ^ bit) for i in range(4)])
+def swap(array, axis):
+    return lax.ppermute(array, axis, [(0, 1), (1, 0)])
 
 
 def shards(densities, amplitudes, partner, qtable, grid_map, coulomb):
-    own = (lax.axis_index("kgrp") * 2).astype(jnp.int32).reshape(1)
-    across = swap(amplitudes, 2)
+    own = (lax.axis_index(KGRP) * 2).astype(jnp.int32).reshape(1)
+    across = swap(amplitudes, "zhi")
     dens = densities.reshape(2, 512, G)
     device = lax.axis_index(AXES)
     received, couls, start = [], [], 0
@@ -182,20 +199,23 @@
         if q == 0:
             sent, across = lax.optimization_barrier((sent, across))
             here = jnp.stack([amplitudes, across])
-            amp = jnp.concatenate([here, swap(here, 1)])
+            amp = jnp.concatenate([here, swap(here, "core")])
         received.append(lax.all_to_all(sent, AXES, 0, 0, tiled=True))
-        couls.append(lax.dynamic_slice(coulomb, (0, start + device * gc), (64, gc)).reshape(-1))
+        couls.append(lax.dynamic_slice(coulomb, (0, start + device * gc), (64, gc)))
         start += 128 * gc
     acc = None
     for q, gc in enumerate(SIZES):
         acc = ladder(own, partner, qtable, couls[q], received[q], amp, acc, q == len(SIZES) - 1, gc)
-    parts = lax.all_to_all(acc.reshape(128, 64, 128), AXES, 0, 0, tiled=True)
+    away, kept = acc
+    both = (kept.astype(F32) + swap(away, "core").astype(F32)).astype(BF)
+    parts = lax.all_to_all(both.reshape(64, 64, 128), ("zhi", "band"), 0, 0, tiled=True)
     total = jnp.sum(parts.astype(F32), axis=0) * (1.0 / math.sqrt(G))
     total = total.astype(BF).reshape(2, 8, 4, 4, 32)
     return jnp.transpose(total, (2, 0, 1, 4, 3)).reshape(4, 2, 8, 128)
 
 
 def solution(mesh):
-    in_specs = (P("kgrp", "band", None, None), P("kgrp", None, None, None), P(), P(), P(), P())
-    out_specs = P("band", "kgrp", None, None)
-    return jax.shard_map(shards, mesh=mesh, in_specs=in_specs, out_specs=out_specs, check_vma=False)
+    split = Mesh(mesh.devices.reshape(2, 2, 32), AXES)
+    in_specs = (P(KGRP, "band", None, None), P(KGRP, None, None, None), P(), P(), P(), P())
+    out_specs = P("band", KGRP, None, None)
+    return jax.shard_map(shards, mesh=split, in_specs=in_specs, out_specs=out_specs, check_vma=False)

time: 199 us -> 190 us (0.955)
  blocking collectives: 35.3 us -> 23.5 us
  waiting for transfers between devices: 60.4 us -> 63 us
    all_to_all x1, blocking collectives: 35.3 us -> 23.5 us  [shards(): lax.all_to_all(both.reshape(64, 64, 128), ('zhi', 'band'), 0, 0, tiled=True)]
    ppermute x2 -> x3, waiting for transfers between devices: 1.2 us -> 4.26 us  [swap(): return lax.ppermute(array, axis, [(0, 1), (1, 0)])]
    ppermute x2 -> x3, starting transfers between devices: 4.05 us -> 4.23 us  [swap(): return lax.ppermute(array, axis, [(0, 1), (1, 0)])]
  transfers between devices with their start and end apart: 4 -> 5, of which waited for: 3 -> 4; matrix products, arithmetic and copies ran while one was open for 2% -> 2% of each run, Pallas kernels for 28% -> 30%
where the time goes in v4:
time: 190 us; the launch traced here: 189 us
  Pallas kernels  77.1 us (41%)
  waiting for transfers between devices  63 us (33%)
  blocking collectives  23.5 us (12%)
  starting transfers between devices  18.5 us (10%)
  other arithmetic  4.62 us (2%)
  local copies, waits for them, and re-layouts  2.39 us (1%)
    all_to_all x2, waiting for transfers between devices, shards(): received.append(lax.all_to_all(sent, AXES, 0, 0, tiled=True))  58.7 us
    pallas_call x2, Pallas kernels, ladder(): pl.pallas_call(functools.partial(ladder_kernel, gc, acc is None, last), g...  50.4 us
    pallas_call x2, Pallas kernels, gather(): pl.pallas_call(functools.partial(gather_kernel, gc, start), grid_spec=plt...  26.7 us
    all_to_all x1, blocking collectives, shards(): lax.all_to_all(both.reshape(64, 64, 128), ('zhi', 'band'), 0, 0, tiled=True)  23.5 us
    all_to_all x2, starting transfers between devices, shards(): received.append(lax.all_to_all(sent, AXES, 0, 0, tiled=True))  14.3 us
    ppermute x3, waiting for transfers between devices, swap(): return lax.ppermute(array, axis, [(0, 1), (1, 0)])  4.26 us
    ppermute x3, starting transfers between devices, swap(): return lax.ppermute(array, axis, [(0, 1), (1, 0)])  4.23 us
  transfers between devices with their start and end apart: 5, of which 4 were waited for; matrix products, arithmetic and copies ran while one was open for 2% of the time, Pallas kernels for 30%

profile of v4, /device:TPU:0, one launch (start us, length us, event | category | flops | bytes accessed | tf_op | source)
XLA Modules:
  0.0 189.3 jit_solution(7408335061176954926)
XLA Ops:
  0.0 0.0 copy-start
  0.0 4.0 %collective-permute-start = (bf16[2,8,128,128]{3,2,1,0:T(8,128)(2,1)}, bf16[2,8,128,128]{3,2,1,0:T(8,128)(2,1)S(1)}, u32[]{:S(2)}, u32[]{:S(2)}) collective-permute-start(bf16[2,8,128,128]{3,2,1,0:T(8,128)(2,1)} %param.7), channel_id=1, source_target_pairs={{0,64},{64,0},{1,65},{65,1},{2,66},{66,2},{3,67},{67,3},{4,68},{68... | collective-permute-start | bytes 1572872 | tf_op jit(solution)/shard_map/ppermute | solution.py:188
  4.0 14.6 %vertex_rows.3 = bf16[128,2,80,128]{3,2,1,0:T(8,128)(2,1)} custom-call(s32[1]{0:T(128)} %bitcast.own_ref, s32[8]{0:T(128)} %qtable_ref.7, s32[64,4096]{1,0:T(8,128)} %map_ref.3, bf16[2,512,4096]{2,1,0:T(8,128)(2,1)} %bitcast.16), custom_call_target="tpu_custom_call" | custom-call | flops 20000000000 | bytes 10000000 | tf_op jit(solution)/shard_map/vertex_rows/pallas_call | solution.py:69
  18.5 0.0 collective-permute-done
  18.6 8.5 %all-to-all-start.1 = ((bf16[128,2,80,128]{3,2,1,0:T(8,128)(2,1)}), bf16[128,2,80,128]{3,2,1,0:T(8,128)(2,1)}, u32[]{:S(2)}, u32[]{:S(2)}) async-start(bf16[128,2,80,128]{3,2,1,0:T(8,128)(2,1)} %vertex_rows.3), calls=%async_computation.1 | async-start | bytes 10485760 | tf_op jit(solution)/shard_map/all_to_all | solution.py:203
  27.1 12.2 %vertex_rows.2 = bf16[128,2,48,128]{3,2,1,0:T(8,128)(2,1)} custom-call(s32[1]{0:T(128)} %bitcast.own_ref, s32[8]{0:T(128)} %qtable_ref.7, s32[64,4096]{1,0:T(8,128)} %map_ref.3, bf16[2,512,4096]{2,1,0:T(8,128)(2,1)} %bitcast.17), custom_call_target="tpu_custom_call" | custom-call | flops 20000000000 | bytes 10000000 | tf_op jit(solution)/shard_map/vertex_rows/pallas_call | solution.py:69
  39.3 0.0 copy-start.1
  39.3 52.8 %all-to-all-done.1 = bf16[128,2,80,128]{3,2,1,0:T(8,128)(2,1)} async-done(((bf16[128,2,80,128]{3,2,1,0:T(8,128)(2,1)}), bf16[128,2,80,128]{3,2,1,0:T(8,128)(2,1)}, u32[]{:S(2)}, u32[]{:S(2)}) %all-to-all-start.1) | async-done | bytes 5242912 | tf_op jit(solution)/shard_map/all_to_all | solution.py:203
  92.1 5.8 %all-to-all-start = ((bf16[128,2,48,128]{3,2,1,0:T(8,128)(2,1)}), bf16[128,2,48,128]{3,2,1,0:T(8,128)(2,1)}, u32[]{:S(2)}, u32[]{:S(2)}) async-start(bf16[128,2,48,128]{3,2,1,0:T(8,128)(2,1)} %vertex_rows.2), calls=%async_computation | async-start | bytes 6291456 | tf_op jit(solution)/shard_map/all_to_all | solution.py:203
  97.9 0.0 copy-done.1
  97.9 0.1 pad_maximum_fusion.1
  98.0 0.3 collective-permute-start.1
  98.3 0.0 copy-done
  98.3 0.7 constant_dynamic-slice_fusion.coul_ref
  99.0 0.7 constant_dynamic-slice_fusion.1.coul_ref
  99.7 1.4 collective-permute-done.1
  101.0 2.7 %pad_maximum_fusion.amp_ref = bf16[4,2,8,128,128]{4,3,2,1,0:T(8,128)(2,1)} fusion(bf16[2,2,8,128,128]{4,3,2,1,0:T(8,128)(2,1)} %collective-permute-done.1, bf16[1,2,8,128,128]{4,3,2,1,0:T(8,128)(2,1)S(1)} %bitcast.13, bf16[1,2,8,128,128]{4,3,2,1,0:T(8,128)(2,1)S(1)} %bitcast.11), kind=kLoop, calls=%fused_computation | loop fusion | flops 2097152 | bytes 4194304 | tf_op jit(solution)/shard_map/concatenate | solution.py:202
  103.8 29.7 %ladder_sum.2.refs_0_ = f32[8,1024,128]{2,1,0:T(8,128)} custom-call(s32[1]{0:T(128)} %bitcast.own_ref, s32[8]{0:T(128)} %partner_ref.3, s32[8]{0:T(128)} %qtable_ref.7, f32[64,20]{1,0:T(8,128)} %constant_dynamic-slice_fusion.coul_ref, bf16[4,32,2,80,128]{4,3,2,1,0:T(8,128)(2,1)} %bitcast.5.recv_ref, bf16[4,2,8,128,128]{4,3,2,1,0:T(8,128)(2,1)} %pad_maximum_fusion.amp_ref), custom_call_target="tpu_custom_call" | custom-call | flops 10737418240 | bytes 12000000 | tf_op jit(solution)/shard_map/ladder_sum/pallas_call | solution.py:175
  133.5 5.9 %all-to-all-done = bf16[128,2,48,128]{3,2,1,0:T(8,128)(2,1)} async-done(((bf16[128,2,48,128]{3,2,1,0:T(8,128)(2,1)}), bf16[128,2,48,128]{3,2,1,0:T(8,128)(2,1)}, u32[]{:S(2)}, u32[]{:S(2)}) %all-to-all-start) | async-done | bytes 3145760 | tf_op jit(solution)/shard_map/all_to_all | solution.py:203
  139.4 20.7 %ladder_sum.3 = (bf16[2,32,2,32,128]{4,3,2,1,0:T(8,128)(2,1)}, bf16[2,32,2,32,128]{4,3,2,1,0:T(8,128)(2,1)}) custom-call(s32[1]{0:T(128)} %bitcast.own_ref, s32[8]{0:T(128)} %partner_ref.3, s32[8]{0:T(128)} %qtable_ref.7, f32[64,12]{1,0:T(8,128)} %constant_dynamic-slice_fusion.1.coul_ref, bf16[4,32,2,48,128]{4,3,2,1,0:T(8,128)(2,1)} %bitcast.2.recv_ref, ...), custom_call_target="tpu_custom_call" | custom-call | flops 6442450944 | bytes 12000000 | tf_op jit(solution)/shard_map/ladder_sum/pallas_call | solution.py:175
  160.1 0.0 collective-permute-start.2
  160.1 2.9 %collective-permute-done.2 = bf16[2,32,2,32,128]{4,3,2,1,0:T(8,128)(2,1)S(1)} collective-permute-done((bf16[2,32,2,32,128]{4,3,2,1,0:T(8,128)(2,1)}, bf16[2,32,2,32,128]{4,3,2,1,0:T(8,128)(2,1)S(1)}, u32[]{:S(2)}, u32[]{:S(2)}) %collective-permute-start.2) | collective-permute-done | bytes 1048608 | tf_op jit(solution)/shard_map/ppermute | solution.py:188
  162.9 1.6 add_convert_fusion
  164.6 23.5 %all_to_all.15 = bf16[64,64,128]{2,1,0:T(8,128)(2,1)S(1)} all-to-all(bf16[64,64,128]{2,1,0:T(8,128)(2,1)S(1)} %bitcast.9), channel_id=1, replica_groups=mesh['zhi'=2,'core'=2,'band'=32] {'zhi','band'}, dimensions={0} | all-to-all | bytes 2097152 | tf_op jit(solution)/shard_map/all_to_all | solution.py:211
  188.1 0.2 convert_reduce_fusion
  188.3 0.1 convert_element_type.24
  188.4 0.2 copy.7
  188.6 0.7 copy.8
  (1 shorter events, 0.0 us)
Async XLA Ops:
  0.0 98.3 %copy-start = (f32[64,4096]{1,0:T(8,128)S(1)}, f32[64,4096]{1,0:T(8,128)}, u32[]{:S(2)}) copy-start(f32[64,4096]{1,0:T(8,128)} %param.11) | copy-start | bytes 3145732
  0.0 18.5 %collective-permute-start = (bf16[2,8,128,128]{3,2,1,0:T(8,128)(2,1)}, bf16[2,8,128,128]{3,2,1,0:T(8,128)(2,1)S(1)}, u32[]{:S(2)}, u32[]{:S(2)}) collective-permute-start(bf16[2,8,128,128]{3,2,1,0:T(8,128)(2,1)} %param.7), channel_id=1, source_target_pairs={{0,64},{64,0},{1,65},{65,1},{2,66},{66,2},{3,67},{67,3},{4,68},{68... | collective-permute-start | bytes 1572872 | tf_op jit(solution)/shard_map/ppermute | solution.py:188
  18.6 73.5 %all-to-all-start.1 = ((bf16[128,2,80,128]{3,2,1,0:T(8,128)(2,1)}), bf16[128,2,80,128]{3,2,1,0:T(8,128)(2,1)}, u32[]{:S(2)}, u32[]{:S(2)}) async-start(bf16[128,2,80,128]{3,2,1,0:T(8,128)(2,1)} %vertex_rows.3), calls=%async_computation.1 | async-start | bytes 10485760 | tf_op jit(solution)/shard_map/all_to_all | solution.py:203
  39.3 58.6 %copy-start.1 = (bf16[2,8,128,128]{3,2,1,0:T(8,128)(2,1)S(1)}, bf16[2,8,128,128]{3,2,1,0:T(8,128)(2,1)}, u32[]{:S(2)}) copy-start(bf16[2,8,128,128]{3,2,1,0:T(8,128)(2,1)} %param.7) | copy-start | bytes 1572868
  92.1 47.3 %all-to-all-start = ((bf16[128,2,48,128]{3,2,1,0:T(8,128)(2,1)}), bf16[128,2,48,128]{3,2,1,0:T(8,128)(2,1)}, u32[]{:S(2)}, u32[]{:S(2)}) async-start(bf16[128,2,48,128]{3,2,1,0:T(8,128)(2,1)} %vertex_rows.2), calls=%async_computation | async-start | bytes 6291456 | tf_op jit(solution)/shard_map/all_to_all | solution.py:203
  98.0 3.1 %collective-permute-start.1 = (bf16[2,2,8,128,128]{4,3,2,1,0:T(8,128)(2,1)S(1)}, bf16[2,2,8,128,128]{4,3,2,1,0:T(8,128)(2,1)}, u32[]{:S(2)}, u32[]{:S(2)}) collective-permute-start(bf16[2,2,8,128,128]{4,3,2,1,0:T(8,128)(2,1)S(1)} %pad_maximum_fusion.1), channel_id=1, source_target_pairs={{0,32},{32,0},{1,33},{33,1},{2,34},{34,2},{3,35},{35,3},{4,36},{36... | collective-permute-start | bytes 3145736 | tf_op jit(solution)/shard_map/ppermute | solution.py:188
  160.1 2.9 %collective-permute-start.2 = (bf16[2,32,2,32,128]{4,3,2,1,0:T(8,128)(2,1)}, bf16[2,32,2,32,128]{4,3,2,1,0:T(8,128)(2,1)S(1)}, u32[]{:S(2)}, u32[]{:S(2)}) collective-permute-start(bf16[2,32,2,32,128]{4,3,2,1,0:T(8,128)(2,1)} %get-tuple-element.12), channel_id=1, source_target_pairs={{0,32},{32,0},{1,33},{33,1},{2,34},{34,2},{3,35},{35,3},{4,36},{36... | collective-permute-start | bytes 3145736 | tf_op jit(solution)/shard_map/ppermute | solution.py:188
